TPU v7x, 32 devices: a whole 2x2x4 slice. The times are simulated.
32 devices in a mesh: dp: 4 (over z), row: 4 (over y, core), col: 2 (over x).
Axes of the slice: x: 2, y: 2, z: 4, core: 2. Of those that a mesh axis runs over, the one named last changes fastest.
Arguments:
- inputs: bfloat16 [8192, 1024], P(('dp', 'row'), 'col'), may hold values from -6 to 6
- cotangent: bfloat16 [8192, 1024], P(('dp', 'row'), 'col'), may hold values from -6 to 6
- norm_gain: float32 [1024], P('col'), may hold values from 0.5 to 1.5
- w_z: bfloat16 [1024, 1536], P('col', 'row'), may hold values from -0.1875 to 0.1875
- w_x: bfloat16 [1024, 1536], P('col', 'row'), may hold values from -0.1875 to 0.1875
- w_dt: bfloat16 [1024, 24], P('col', 'row'), may hold values from -0.09375 to 0.09375
- w_bc: bfloat16 [1024, 256], P('col'), may hold values from -0.1875 to 0.1875
- conv_x: bfloat16 [4, 1536], P(None, ('row', 'col')), may hold values from -3 to 3
- bias_x: float32 [1536], P(('row', 'col')), may hold values from -3 to 3
- conv_bc: bfloat16 [4, 256], replicated, may hold values from -3 to 3
- bias_bc: float32 [256], replicated, may hold values from -3 to 3
- dt_bias: float32 [24], P(('row', 'col')), may hold values from -4.5 to -2
- a_log: float32 [24], P(('row', 'col')), may hold values from 0 to 2.8
- d_skip: float32 [24], P(('row', 'col')), may hold values from 0.5 to 1.5
- mixer_gain: float32 [1536], P(('row', 'col')), may hold values from 0.5 to 1.5
- out_mamba: bfloat16 [1536, 1024], P('row', 'col'), may hold values from -0.15625 to 0.15625
- w_query: bfloat16 [1024, 512], P('col', 'row'), may hold values from -0.1875 to 0.1875
- key_matrix: bfloat16 [1024, 128], P('col'), may hold values from -0.1875 to 0.1875
- value_matrix: bfloat16 [1024, 128], P('col'), may hold values from -0.1875 to 0.1875
- out_attn: bfloat16 [512, 1024], P('row', 'col'), may hold values from -0.75 to 0.75
- ffn_gain: float32 [1024], P('col'), may hold values from 0.5 to 1.5
- w_gate: bfloat16 [1024, 2048], P('col', 'row'), may hold values from -0.1875 to 0.1875
- w_up: bfloat16 [1024, 2048], P('col', 'row'), may hold values from -0.1875 to 0.1875
- w_down: bfloat16 [2048, 1024], P('row', 'col'), may hold values from -0.125 to 0.125
Outputs:
- block_out: bfloat16 [8192, 1024], P(('dp', 'row'), 'col')
- grad_inputs: float32 [8192, 1024], P(('dp', 'row'), 'col')
- grad_norm_gain: float32 [1024], P('col')
- grad_w_z: float32 [1024, 1536], P('col', 'row')
- grad_w_x: float32 [1024, 1536], P('col', 'row')
- grad_w_dt: float32 [1024, 24], P('col', 'row')
- grad_w_bc: float32 [1024, 256], P('col')
- grad_conv_x: float32 [4, 1536], P(None, ('row', 'col'))
- grad_bias_x: float32 [1536], P(('row', 'col'))
- grad_conv_bc: float32 [4, 256], replicated
- grad_bias_bc: float32 [256], replicated
- grad_dt_bias: float32 [24], P(('row', 'col'))
- grad_a_log: float32 [24], P(('row', 'col'))
- grad_d_skip: float32 [24], P(('row', 'col'))
- grad_mixer_gain: float32 [1536], P(('row', 'col'))
- grad_out_mamba: float32 [1536, 1024], P('row', 'col')
- grad_w_query: float32 [1024, 512], P('col', 'row')
- key_weight_gradient: float32 [1024, 128], P('col')
- value_weight_gradient: float32 [1024, 128], P('col')
- grad_out_attn: float32 [512, 1024], P('row', 'col')
- grad_ffn_gain: float32 [1024], P('col')
- grad_w_gate: float32 [1024, 2048], P('col', 'row')
- grad_w_up: float32 [1024, 2048], P('col', 'row')
- grad_w_down: float32 [2048, 1024], P('row', 'col')
All inputs are finite; a program needn't handle non-finite values.
Results may differ from a plain program's by a relative error of at most 0.035.
Values may be sent and summed in bfloat16 or wider, within the bound.
A program may use at most 128 MiB of HBM per device.

v0:
```python
from functools import partial
import math

import jax
import jax.numpy as jnp
from jax import lax
from jax.sharding import PartitionSpec as P

MODEL_WIDTH = 1024
STATE_SIZE = 128
KC = 4
QUERY_HEADS = 8
KEY_VALUE_HEADS = 2
HEAD_SIZE = 64
CH = 128
QB = 512
DM = 1536


epsilon = 1e-05
rope_base = 100000000000.0
masked_score = -1e30
highest = lax.Precision.HIGHEST


def causal_conv(raw, kernel, offset):
    sequence_length = raw.shape[0]
    padded = jnp.pad(raw, ((KC - 1, 0), (0, 0)))
    summed = offset + kernel[0] * padded[0:sequence_length]
    for tap_index in range(1, KC):
        summed = summed + kernel[tap_index] * padded[tap_index : tap_index + sequence_length]
    return jax.nn.silu(summed)


def apply_rotary(values, token_positions):
    half_width = values.shape[-1] // 2
    frequency = jnp.exp(
        jnp.arange(half_width).astype(jnp.float32) * (-2.0 * math.log(rope_base) / values.shape[-1])
    )
    angle_half = token_positions[:, None] * frequency[None, :]
    angle_full = jnp.concatenate([angle_half, angle_half], axis=-1)[:, None, :]
    turned = jnp.concatenate([-values[..., half_width:], values[..., :half_width]], axis=-1)
    return values * jnp.cos(angle_full) + turned * jnp.sin(angle_full)


def state_scan(values, b_rows, c_rows, step_sizes, log_decay):
    sequence_length, head_count, head_width = values.shape
    states = b_rows.shape[1]
    blocks = sequence_length // CH
    grouped = (
        values.reshape(blocks, CH, head_count, head_width),
        b_rows.reshape(blocks, CH, states),
        c_rows.reshape(blocks, CH, states),
        step_sizes.reshape(blocks, CH, head_count),
        log_decay.reshape(blocks, CH, head_count),
    )
    position = jnp.arange(CH, dtype=jnp.int32)
    causal = (position[:, None] >= position[None, :])[:, :, None]

    def advance(carry_state, block_in):
        block_values, b_block, c_block, step_block, decay_block = block_in
        cumulative = jnp.cumsum(decay_block, axis=0)
        within = jnp.exp(
            jnp.where(causal, cumulative[:, None, :] - cumulative[None, :, :], masked_score)
        )
        scores = jnp.dot(
            c_block.astype(jnp.bfloat16),
            b_block.astype(jnp.bfloat16).T,
            preferred_element_type=jnp.float32,
        )
        mixing = within * scores[:, :, None] * step_block[None, :, :]
        inside = jnp.einsum("ijh,jhp->ihp", mixing, block_values, precision=highest)
        carried = (
            jnp.einsum("hpn,in->ihp", carry_state, c_block, precision=highest)
            * jnp.exp(cumulative)[:, :, None]
        )
        tail_weight = jnp.exp(cumulative[-1][None, :] - cumulative) * step_block
        carry_state = jnp.exp(cumulative[-1])[:, None, None] * carry_state + jnp.einsum(
            "jh,jhp,jn->hpn", tail_weight, block_values, b_block, precision=highest
        )
        return (carry_state, inside + carried)

    initial = jnp.zeros((head_count, head_width, states), values.dtype)
    _, outputs = lax.scan(jax.checkpoint(advance), initial, grouped)
    return outputs.reshape(sequence_length, head_count, head_width)


def mixer_core(conv_values, b_rows, c_rows, dt_raw, dt_bias, a_log, d_skip):
    sequence_length = conv_values.shape[0]
    head_count = dt_bias.shape[0]
    per_head = conv_values.reshape(sequence_length, head_count, -1)
    step_sizes = jax.nn.softplus(dt_raw + dt_bias)
    log_decay = -step_sizes * jnp.exp(a_log)
    output = (
        state_scan(per_head, b_rows, c_rows, step_sizes, log_decay) + d_skip[:, None] * per_head
    )
    return output.reshape(sequence_length, -1)


def silu_slope(values):
    sigmoid = jax.nn.sigmoid(values)
    return sigmoid * (1.0 + values * (1.0 - sigmoid))


def col_total(values):
    return lax.psum(values, "col")


def gather_rows(values):
    return lax.all_gather(values, "row", axis=0, tiled=True)


def rows_total(values):
    return lax.psum_scatter(values, "row", scatter_dimension=0, tiled=True)


def cols_total(values):
    return lax.psum_scatter(
        values.astype(jnp.bfloat16), "col", scatter_dimension=1, tiled=True
    ).astype(jnp.float32)


def gather_cols(values):
    return lax.all_gather(values, "col", axis=1, tiled=True)


def grid_total(values):
    return lax.psum(values, ("row", "col"))


def norm_forward(values, gain):
    squares = col_total(jnp.sum(values * values, axis=-1))
    scale_row = lax.rsqrt(squares / MODEL_WIDTH + epsilon)
    return (values * scale_row[:, None] * gain, scale_row)


def norm_backward(values, scale_row, gain, grad_out):
    weighted = gain * grad_out
    inner_sum = col_total(jnp.sum(weighted * values, axis=-1))
    grad_in = (
        scale_row[:, None] * weighted - values * (scale_row**3 * inner_sum / MODEL_WIDTH)[:, None]
    )
    return (grad_in, jnp.sum(grad_out * values * scale_row[:, None], axis=0))


def block_scores(queries, key_rows, first, sequence_length):
    query_blk = lax.dynamic_slice_in_dim(queries, first, QB, 0)
    scores = jnp.einsum(
        "qd,kd->qk", query_blk, key_rows, preferred_element_type=jnp.float32
    ) * HEAD_SIZE ** (-0.5)
    query_pos = first + jnp.arange(QB)
    key_pos = jnp.arange(sequence_length)
    return (query_blk, jnp.where(key_pos[None, :] <= query_pos[:, None], scores, masked_score))


def attend_forward(queries, key_rows, value_input, sequence_length):

    def block_out(first):
        _, scores = block_scores(queries, key_rows, first, sequence_length)
        peak = jnp.max(scores, axis=-1, keepdims=True)
        shifted = jnp.exp(scores - peak)
        total_sum = jnp.sum(shifted, axis=-1, keepdims=True)
        weights = (shifted / total_sum).astype(jnp.bfloat16)
        output = jnp.einsum("qk,kd->qd", weights, value_input, preferred_element_type=jnp.float32)
        return (output, (peak + jnp.log(total_sum))[:, 0])

    outputs, log_totals = lax.map(block_out, jnp.arange(sequence_length // QB) * QB)
    return (outputs.reshape(sequence_length, -1), log_totals.reshape(sequence_length))


def attend_backward(queries, key_rows, value_input, grad_low, log_totals, sequence_length):

    def block_grad(carry, first):
        grad_keys, grad_values = carry
        query_blk, scores = block_scores(queries, key_rows, first, sequence_length)
        grad_blk = lax.dynamic_slice_in_dim(grad_low, first, QB, 0)
        log_blk = lax.dynamic_slice_in_dim(log_totals, first, QB, 0)
        probs = jnp.exp(scores - log_blk[:, None])
        grad_probs = jnp.einsum(
            "qd,kd->qk", grad_blk, value_input, preferred_element_type=jnp.float32
        )
        centre = jnp.sum(probs * grad_probs, axis=-1, keepdims=True)
        grad_scores = (probs * (grad_probs - centre)).astype(jnp.bfloat16)
        grad_query = jnp.einsum(
            "qk,kd->qd", grad_scores, key_rows, preferred_element_type=jnp.float32
        ) * HEAD_SIZE ** (-0.5)
        grad_keys = grad_keys + jnp.einsum(
            "qk,qd->kd", grad_scores, query_blk, preferred_element_type=jnp.float32
        ) * HEAD_SIZE ** (-0.5)
        grad_values = grad_values + jnp.einsum(
            "qk,qd->kd", probs.astype(jnp.bfloat16), grad_blk, preferred_element_type=jnp.float32
        )
        return ((grad_keys, grad_values), grad_query)

    zero_rows = jnp.zeros((sequence_length, key_rows.shape[1]), jnp.float32)
    (grad_keys, grad_values), grad_queries = lax.scan(
        block_grad, (zero_rows, zero_rows), jnp.arange(sequence_length // QB) * QB
    )
    return (grad_queries.reshape(sequence_length, -1), grad_keys, grad_values)


def local(
    inputs,
    cotangent,
    norm_gain,
    w_z,
    w_x,
    w_dt,
    w_bc,
    conv_x,
    bias_x,
    conv_bc,
    bias_bc,
    dt_bias,
    a_log,
    d_skip,
    mixer_gain,
    out_mamba,
    w_query,
    key_matrix,
    value_matrix,
    out_attn,
    ffn_gain,
    w_gate,
    w_up,
    w_down,
):
    col_count = lax.axis_size("col")
    row_count = lax.axis_size("row")
    row_index = lax.axis_index("row")
    device_position = row_index * col_count + lax.axis_index("col")
    rows_local = inputs.shape[0]
    sequence_length = rows_local * row_count
    x_width = conv_x.shape[1]
    ffn_local = w_down.shape[0] // col_count
    segment = 2 * x_width + HEAD_SIZE
    out_segment = x_width + HEAD_SIZE
    single_float = jnp.float32
    bf16 = jnp.bfloat16
    main_parts = []
    out_parts = []
    ffn_parts = []
    for column in range(col_count):
        main_parts += [
            w_z[:, column * x_width : (column + 1) * x_width],
            w_x[:, column * x_width : (column + 1) * x_width],
            w_query[:, column * HEAD_SIZE : (column + 1) * HEAD_SIZE],
        ]
        out_parts += [
            out_mamba[column * x_width : (column + 1) * x_width],
            out_attn[column * HEAD_SIZE : (column + 1) * HEAD_SIZE],
        ]
        ffn_parts += [
            w_gate[:, column * ffn_local : (column + 1) * ffn_local],
            w_up[:, column * ffn_local : (column + 1) * ffn_local],
        ]
    w_main = jnp.concatenate(main_parts, axis=1)
    w_out = jnp.concatenate(out_parts, axis=0)
    w_ffn = jnp.concatenate(ffn_parts, axis=1)
    key_value_head = device_position // (QUERY_HEADS // KEY_VALUE_HEADS)
    key_part = lax.dynamic_slice_in_dim(key_matrix, key_value_head * HEAD_SIZE, HEAD_SIZE, 1)
    value_part = lax.dynamic_slice_in_dim(value_matrix, key_value_head * HEAD_SIZE, HEAD_SIZE, 1)
    w_shared = jnp.concatenate([w_bc, key_part, value_part], axis=1)
    w_shared_full = jnp.concatenate([w_bc, key_matrix, value_matrix], axis=1)
    x_float = inputs.astype(single_float)
    normed, scale_one = norm_forward(x_float, norm_gain)
    normed_low = normed.astype(bf16)
    normed_all = gather_rows(normed_low)
    main_term = jnp.dot(normed_all, w_main, preferred_element_type=single_float)
    dt_term = jnp.dot(normed_all, w_dt, preferred_element_type=single_float)
    shared_term = jnp.dot(normed_all, w_shared, preferred_element_type=single_float)
    main_sum, dt_raw, shared_stack = (
        lax.psum_scatter(main_term, "col", scatter_dimension=1, tiled=True),
        lax.psum_scatter(dt_term, "col", scatter_dimension=1, tiled=True),
        lax.psum_scatter(
            jnp.broadcast_to(shared_term[None], (col_count,) + shared_term.shape),
            "col",
            scatter_dimension=0,
            tiled=True,
        ),
    )
    shared_sum = shared_stack[0]
    gate_z = main_sum[:, :x_width]
    x_raw = main_sum[:, x_width : 2 * x_width]
    q_raw = main_sum[:, 2 * x_width :]
    bc_raw = shared_sum[:, : 2 * STATE_SIZE]
    key_unrotated = shared_sum[:, 2 * STATE_SIZE : 2 * STATE_SIZE + HEAD_SIZE]
    value_unprojected = shared_sum[:, 2 * STATE_SIZE + HEAD_SIZE :]
    x_conv, x_conv_pull = jax.vjp(causal_conv, x_raw, conv_x.astype(single_float), bias_x)
    bc_conv, bc_conv_pull = jax.vjp(causal_conv, bc_raw, conv_bc.astype(single_float), bias_bc)
    x_low = lax.optimization_barrier(x_conv.astype(bf16)).astype(single_float)
    bc_low = lax.optimization_barrier(bc_conv.astype(bf16)).astype(single_float)
    ssm_out, core_pull = jax.vjp(
        mixer_core,
        x_low,
        bc_low[:, :STATE_SIZE],
        bc_low[:, STATE_SIZE:],
        dt_raw,
        dt_bias,
        a_log,
        d_skip,
    )
    gated = ssm_out * jax.nn.silu(gate_z)
    mixer_scale = lax.rsqrt(grid_total(jnp.sum(gated * gated, axis=-1)) / DM + epsilon)
    mixed_low = (gated * mixer_scale[:, None] * mixer_gain).astype(bf16)
    token_positions = jnp.arange(sequence_length).astype(single_float)
    q_rot, q_pull = jax.vjp(
        partial(apply_rotary, token_positions=token_positions),
        q_raw.reshape(sequence_length, 1, HEAD_SIZE),
    )
    key_rotated, k_pull = jax.vjp(
        partial(apply_rotary, token_positions=token_positions),
        key_unrotated.reshape(sequence_length, 1, HEAD_SIZE),
    )
    q_low = q_rot.reshape(sequence_length, HEAD_SIZE).astype(bf16)
    k_low = key_rotated.reshape(sequence_length, HEAD_SIZE).astype(bf16)
    value_reduced = value_unprojected.astype(bf16)
    attn_out, log_totals = attend_forward(q_low, k_low, value_reduced, sequence_length)
    attn_low = attn_out.astype(bf16)
    joined = gather_cols(jnp.concatenate([mixed_low, attn_low], axis=1))
    middle = x_float + rows_total(jnp.dot(joined, w_out, preferred_element_type=single_float))
    normed_ffn, scale_two = norm_forward(middle, ffn_gain)
    ffn_all = gather_rows(normed_ffn.astype(bf16))
    gate_up = cols_total(jnp.dot(ffn_all, w_ffn, preferred_element_type=single_float))
    gate_ffn = gate_up[:, :ffn_local]
    up_ffn = gate_up[:, ffn_local:]
    gate_silu = jax.nn.silu(gate_ffn)
    act_all = gather_cols((gate_silu * up_ffn).astype(bf16))
    block_out = middle + rows_total(jnp.dot(act_all, w_down, preferred_element_type=single_float))
    grad_out = cotangent.astype(single_float)
    grad_ffn_all = gather_rows(cotangent)
    grad_w_down = jnp.einsum(
        "tf,td->fd", act_all, grad_ffn_all, preferred_element_type=single_float
    )
    grad_act = cols_total(
        jnp.einsum("td,fd->tf", grad_ffn_all, w_down, preferred_element_type=single_float)
    )
    grad_gate = grad_act * up_ffn * silu_slope(gate_ffn)
    grad_up = grad_act * gate_silu
    grad_ffn_cols = gather_cols(jnp.concatenate([grad_gate, grad_up], axis=1).astype(bf16))
    grad_w_ffn = jnp.einsum(
        "td,tk->dk", ffn_all, grad_ffn_cols, preferred_element_type=single_float
    )
    grad_ffn_in = rows_total(
        jnp.einsum("tk,dk->td", grad_ffn_cols, w_ffn, preferred_element_type=single_float)
    )
    grad_middle_norm, grad_ffn_gain = norm_backward(middle, scale_two, ffn_gain, grad_ffn_in)
    grad_middle = grad_out + grad_middle_norm
    grad_branch_all = gather_rows(grad_middle.astype(bf16))
    grad_w_out = jnp.einsum(
        "tk,td->kd", joined, grad_branch_all, preferred_element_type=single_float
    )
    grad_joined = cols_total(
        jnp.einsum("td,kd->tk", grad_branch_all, w_out, preferred_element_type=single_float)
    )
    grad_mixed = grad_joined[:, :x_width]
    grad_attn = grad_joined[:, x_width:].astype(bf16)
    grad_q_rot, grad_k_rot, value_gradient = attend_backward(
        q_low, k_low, value_reduced, grad_attn, log_totals, sequence_length
    )
    grad_q = q_pull(grad_q_rot.reshape(sequence_length, 1, HEAD_SIZE))[0].reshape(
        sequence_length, HEAD_SIZE
    )
    key_gradient = k_pull(grad_k_rot.reshape(sequence_length, 1, HEAD_SIZE))[0].reshape(
        sequence_length, HEAD_SIZE
    )
    weighted = mixer_gain * grad_mixed
    inner_sum = grid_total(jnp.sum(weighted * gated, axis=-1))
    grad_gated = (
        mixer_scale[:, None] * weighted - gated * (mixer_scale**3 * inner_sum / DM)[:, None]
    )
    grad_mixer_gain = jnp.sum(grad_mixed * gated * mixer_scale[:, None], axis=0)
    grad_ssm = grad_gated * jax.nn.silu(gate_z)
    grad_z = grad_gated * ssm_out * silu_slope(gate_z)
    grad_xc, grad_b, grad_c, grad_dt, grad_dt_bias, grad_a_log, grad_d_skip = core_pull(grad_ssm)
    grad_x_raw, grad_conv_x, grad_bias_x = x_conv_pull(grad_xc)
    head_selection = (jnp.arange(KEY_VALUE_HEADS) == key_value_head).astype(single_float)
    key_gradient_padded = (head_selection[None, :, None] * key_gradient[:, None, :]).reshape(
        sequence_length, KEY_VALUE_HEADS * HEAD_SIZE
    )
    value_gradient_padded = (head_selection[None, :, None] * value_gradient[:, None, :]).reshape(
        sequence_length, KEY_VALUE_HEADS * HEAD_SIZE
    )
    grad_bc_sum, grad_k_sum, grad_v_sum = (
        lax.psum(
            jnp.concatenate([grad_b, grad_c], axis=1).astype(jnp.bfloat16), ("row", "col")
        ).astype(jnp.float32),
        lax.psum(key_gradient_padded.astype(jnp.bfloat16), ("row", "col")).astype(jnp.float32),
        lax.psum(value_gradient_padded.astype(jnp.bfloat16), ("row", "col")).astype(jnp.float32),
    )
    grad_bc_raw, grad_conv_bc, grad_bias_bc = bc_conv_pull(grad_bc_sum)
    grad_shared = jnp.concatenate([grad_bc_raw, grad_k_sum, grad_v_sum], axis=1).astype(bf16)
    grad_main_all, grad_dt_all = (
        lax.all_gather(
            jnp.concatenate([grad_z, grad_x_raw, grad_q], axis=1).astype(bf16),
            "col",
            axis=1,
            tiled=True,
        ),
        lax.all_gather(grad_dt.astype(bf16), "col", axis=1, tiled=True),
    )
    grad_w_main = jnp.einsum(
        "td,tk->dk", normed_all, grad_main_all, preferred_element_type=single_float
    )
    grad_w_dt = jnp.einsum(
        "td,tk->dk", normed_all, grad_dt_all, preferred_element_type=single_float
    )
    grad_normed = rows_total(
        jnp.einsum("tk,dk->td", grad_main_all, w_main, preferred_element_type=single_float)
        + jnp.einsum("tk,dk->td", grad_dt_all, w_dt, preferred_element_type=single_float)
    )
    own_shared = lax.dynamic_slice_in_dim(grad_shared, row_index * rows_local, rows_local, 0)
    grad_normed = grad_normed + jnp.einsum(
        "tk,dk->td", own_shared, w_shared_full, preferred_element_type=single_float
    )
    grad_x_norm, grad_norm_gain = norm_backward(x_float, scale_one, norm_gain, grad_normed)
    grad_inputs = grad_middle + grad_x_norm
    z_list = []
    x_list = []
    q_list = []
    mamba_list = []
    attn_list = []
    gate_list = []
    up_list = []
    for column in range(col_count):
        base_main = column * segment
        z_list.append(grad_w_main[:, base_main : base_main + x_width])
        x_list.append(grad_w_main[:, base_main + x_width : base_main + 2 * x_width])
        q_list.append(grad_w_main[:, base_main + 2 * x_width : base_main + segment])
        base_out = column * out_segment
        mamba_list.append(grad_w_out[base_out : base_out + x_width])
        attn_list.append(grad_w_out[base_out + x_width : base_out + out_segment])
        base_ffn = column * 2 * ffn_local
        gate_list.append(grad_w_ffn[:, base_ffn : base_ffn + ffn_local])
        up_list.append(grad_w_ffn[:, base_ffn + ffn_local : base_ffn + 2 * ffn_local])
    grad_w_z = jnp.concatenate(z_list, axis=1)
    grad_w_x = jnp.concatenate(x_list, axis=1)
    grad_w_query = jnp.concatenate(q_list, axis=1)
    grad_out_mamba = jnp.concatenate(mamba_list, axis=0)
    grad_out_attn = jnp.concatenate(attn_list, axis=0)
    grad_w_gate = jnp.concatenate(gate_list, axis=1)
    grad_w_up = jnp.concatenate(up_list, axis=1)
    shared_weight_gradient = jnp.einsum(
        "td,tk->dk", normed_all, grad_shared, preferred_element_type=single_float
    )
    (
        grad_w_z,
        grad_w_x,
        grad_w_dt,
        grad_conv_x,
        grad_bias_x,
        grad_dt_bias,
        grad_a_log,
        grad_d_skip,
        grad_mixer_gain,
        grad_out_mamba,
        grad_w_query,
        grad_out_attn,
        grad_w_gate,
        grad_w_up,
        grad_w_down,
        shared_weight_gradient,
        grad_conv_bc,
        grad_bias_bc,
    ) = (
        lax.psum(grad_w_z.astype(jnp.bfloat16), "dp").astype(jnp.float32),
        lax.psum(grad_w_x.astype(jnp.bfloat16), "dp").astype(jnp.float32),
        lax.psum(grad_w_dt.astype(jnp.bfloat16), "dp").astype(jnp.float32),
        lax.psum(grad_conv_x.astype(jnp.bfloat16), "dp").astype(jnp.float32),
        lax.psum(grad_bias_x.astype(jnp.bfloat16), "dp").astype(jnp.float32),
        lax.psum(grad_dt_bias.astype(jnp.bfloat16), "dp").astype(jnp.float32),
        lax.psum(grad_a_log.astype(jnp.bfloat16), "dp").astype(jnp.float32),
        lax.psum(grad_d_skip.astype(jnp.bfloat16), "dp").astype(jnp.float32),
        lax.psum(grad_mixer_gain.astype(jnp.bfloat16), "dp").astype(jnp.float32),
        lax.psum(grad_out_mamba.astype(jnp.bfloat16), "dp").astype(jnp.float32),
        lax.psum(grad_w_query.astype(jnp.bfloat16), "dp").astype(jnp.float32),
        lax.psum(grad_out_attn.astype(jnp.bfloat16), "dp").astype(jnp.float32),
        lax.psum(grad_w_gate.astype(jnp.bfloat16), "dp").astype(jnp.float32),
        lax.psum(grad_w_up.astype(jnp.bfloat16), "dp").astype(jnp.float32),
        lax.psum(grad_w_down.astype(jnp.bfloat16), "dp").astype(jnp.float32),
        lax.psum(shared_weight_gradient.astype(jnp.bfloat16), "dp").astype(jnp.float32),
        lax.psum(grad_conv_bc.astype(jnp.bfloat16), "dp").astype(jnp.float32),
        lax.psum(grad_bias_bc.astype(jnp.bfloat16), "dp").astype(jnp.float32),
    )
    grad_norm_gain, grad_ffn_gain = lax.psum((grad_norm_gain, grad_ffn_gain), ("dp", "row"))
    grad_w_bc = shared_weight_gradient[:, : 2 * STATE_SIZE]
    key_weight_gradient = shared_weight_gradient[
        :, 2 * STATE_SIZE : 2 * STATE_SIZE + KEY_VALUE_HEADS * HEAD_SIZE
    ]
    value_weight_gradient = shared_weight_gradient[
        :, 2 * STATE_SIZE + KEY_VALUE_HEADS * HEAD_SIZE :
    ]
    return (
        block_out.astype(bf16),
        grad_inputs,
        grad_norm_gain,
        grad_w_z,
        grad_w_x,
        grad_w_dt,
        grad_w_bc,
        grad_conv_x,
        grad_bias_x,
        grad_conv_bc,
        grad_bias_bc,
        grad_dt_bias,
        grad_a_log,
        grad_d_skip,
        grad_mixer_gain,
        grad_out_mamba,
        grad_w_query,
        key_weight_gradient,
        value_weight_gradient,
        grad_out_attn,
        grad_ffn_gain,
        grad_w_gate,
        grad_w_up,
        grad_w_down,
    )


def solution(mesh):
    in_specs = (
        P(("dp", "row"), "col"),
        P(("dp", "row"), "col"),
        P("col"),
        P("col", "row"),
        P("col", "row"),
        P("col", "row"),
        P("col", None),
        P(None, ("row", "col")),
        P(("row", "col")),
        P(),
        P(),
        P(("row", "col")),
        P(("row", "col")),
        P(("row", "col")),
        P(("row", "col")),
        P("row", "col"),
        P("col", "row"),
        P("col", None),
        P("col", None),
        P("row", "col"),
        P("col"),
        P("col", "row"),
        P("col", "row"),
        P("row", "col"),
    )
    out_specs = (
        P(("dp", "row"), "col"),
        P(("dp", "row"), "col"),
        P("col"),
        P("col", "row"),
        P("col", "row"),
        P("col", "row"),
        P("col", None),
        P(None, ("row", "col")),
        P(("row", "col")),
        P(),
        P(),
        P(("row", "col")),
        P(("row", "col")),
        P(("row", "col")),
        P(("row", "col")),
        P("row", "col"),
        P("col", "row"),
        P("col", None),
        P("col", None),
        P("row", "col"),
        P("col"),
        P("col", "row"),
        P("col", "row"),
        P("row", "col"),
    )
    return jax.shard_map(local, mesh=mesh, in_specs=in_specs, out_specs=out_specs, check_vma=False)
```

profile of v0, /device:TPU:0, one launch (start us, length us, event | category | flops | bytes accessed | tf_op | source)
XLA Modules:
  0.0 1735.9 jit_solution(13435437678330459106)
XLA Ops:
  8.6 5.8 psum.203
  17.4 24.2 %all-gather.10.cloned.1.call-done = bf16[2048,512]{1,0:T(8,128)(2,1)} async-done(((bf16[512,512]{1,0:T(8,128)(2,1)}), bf16[2048,512]{1,0:T(8,128)(2,1)}) %all-gather.10.cloned.1.call-update) | async-done | bytes 2097168 | tf_op jit(solution)/shard_map/all_gather | solution.py:110
  55.9 6.2 fusion.215
  66.8 10.4 all-reduce.24
  80.1 46.5 %reduce-scatter.12.cloned.1.call-done = f32[1,2048,384]{1,2,0:T(8,128)} async-done(((f32[2,2048,384]{1,2,0:T(8,128)}), f32[1,2048,384]{1,2,0:T(8,128)}) %reduce-scatter.12.cloned.1.call-update) | async-done | bytes 3145744 | tf_op jit(solution)/shard_map/reduce_scatter | solution.py:275
  131.3 7.0 multiply_convert_fusion.2
  144.5 73.0 %reduce-scatter.10.cloned.1.call-done = f32[2048,448]{0,1:T(8,128)} async-done(((f32[2048,896]{0,1:T(8,128)}), f32[2048,448]{0,1:T(8,128)}) %reduce-scatter.10.cloned.1.call-update) | async-done | bytes 3670032 | tf_op jit(solution)/shard_map/reduce_scatter | solution.py:273
  222.7 31.7 %while.68 = (s32[]{:T(128)}, bf16[4,512,64]{1,2,0:T(8,128)(2,1)S(1)}, f32[4,512]{1,0:T(4,128)}, s32[4]{0:T(128)}, bf16[2048,64]{1,0:T(8,128)(2,1)S(1)}, /*index=...) while((s32[]{:T(128)}, ...), condition=%wide.region_13.14_spmd, body=%wide.region_10.13_spmd.sunk | while | flops 277872640 | bytes 13918379 | solution.py:167
  262.1 153.7 %while.69 = (s32[]{:T(128)}, f32[3,64,128]{2,1,0:T(8,128)S(1)}, f32[16,128,3,64]{1,0,3,2:T(8,128)S(1)}, f32[16,3,64,128]{3,2,1,0:T(8,128)}, f32[16,128,3]{2,1,0:...) while((s32[]{:T(128)}, f32[3,64,128]{2,1,0:T(8,128)S(1)}, ...), condition=%wide.region_7.8_spmd.clone, body=%wide.region_5.7_spmd.clone.sunk | while | flops 117883264 | bytes 1561844 | solution.py:84
  420.2 13.3 psum.204
  436.0 32.8 %all-gather.12.cloned.1.call-done = bf16[2048,512]{0,1:T(8,128)(2,1)} async-done(((bf16[2048,256]{0,1:T(8,128)(2,1)}), bf16[2048,512]{0,1:T(8,128)(2,1)}) %all-gather.12.cloned.1.call-update) | async-done | bytes 2097168 | tf_op jit(solution)/shard_map/all_gather | solution.py:124
  473.8 44.6 %reduce-scatter.14.cloned.1.call-done = f32[512,512]{1,0:T(8,128)} async-done(((f32[2048,512]{1,0:T(8,128)}), f32[512,512]{1,0:T(8,128)}) %reduce-scatter.14.cloned.1.call-update) | async-done | bytes 1048592 | tf_op jit(solution)/shard_map/reduce_scatter | solution.py:114
  527.6 21.1 %all-gather.14.cloned.1.call-done = bf16[2048,512]{1,0:T(8,128)(2,1)} async-done(((bf16[512,512]{1,0:T(8,128)(2,1)}), bf16[2048,512]{1,0:T(8,128)(2,1)}) %all-gather.14.cloned.1.call-update) | async-done | bytes 2097168 | tf_op jit(solution)/shard_map/all_gather | solution.py:110
  548.7 6.0 convolution_convert_fusion.2
  554.8 18.1 %all-gather.18.cloned.1.call-done = bf16[2048,512]{1,0:T(8,128)(2,1)} async-done(((bf16[512,512]{1,0:T(8,128)(2,1)}), bf16[2048,512]{1,0:T(8,128)(2,1)}) %all-gather.18.cloned.1.call-update) | async-done | bytes 2097168 | tf_op jit(solution)/shard_map/all_gather | solution.py:110
  577.2 52.5 %reduce-scatter.16.cloned.1.call-done = bf16[2048,512]{0,1:T(8,128)(2,1)} async-done(((bf16[2048,1024]{0,1:T(8,128)(2,1)}), bf16[2048,512]{0,1:T(8,128)(2,1)}) %reduce-scatter.16.cloned.1.call-update) | async-done | bytes 2097168 | tf_op jit(solution)/shard_map/reduce_scatter | solution.py:118
  633.8 30.0 %reduce-scatter.20.cloned.1.call-done = bf16[2048,256]{0,1:T(8,128)(2,1)} async-done(((bf16[2048,512]{0,1:T(8,128)(2,1)}), bf16[2048,256]{0,1:T(8,128)(2,1)}) %reduce-scatter.20.cloned.1.call-update) | async-done | bytes 1048592 | tf_op jit(solution)/shard_map/reduce_scatter | solution.py:118
  670.4 56.9 %all-gather.20.cloned.1.call-done = bf16[2048,1024]{0,1:T(8,128)(2,1)} async-done(((bf16[2048,512]{0,1:T(8,128)(2,1)}), bf16[2048,1024]{0,1:T(8,128)(2,1)}) %all-gather.20.cloned.1.call-update) | async-done | bytes 4194320 | tf_op jit(solution)/shard_map/all_gather | solution.py:124
  727.3 6.6 fusion.168
  734.0 44.6 %reduce-scatter.22.cloned.1.call-done = f32[512,512]{1,0:T(8,128)} async-done(((f32[2048,512]{1,0:T(8,128)}), f32[512,512]{1,0:T(8,128)}) %reduce-scatter.22.cloned.1.call-update) | async-done | bytes 1048592 | tf_op jit(solution)/shard_map/reduce_scatter | solution.py:114
  789.4 21.9 %all-gather.22.cloned.1.call-done = bf16[2048,512]{1,0:T(8,128)(2,1)} async-done(((bf16[512,512]{1,0:T(8,128)(2,1)}), bf16[2048,512]{1,0:T(8,128)(2,1)}) %all-gather.22.cloned.1.call-update) | async-done | bytes 2097168 | tf_op jit(solution)/shard_map/all_gather | solution.py:110
  818.1 27.9 %all-gather.16.cloned.1.call-done = bf16[2048,512]{0,1:T(8,128)(2,1)} async-done(((bf16[2048,256]{0,1:T(8,128)(2,1)}), bf16[2048,512]{0,1:T(8,128)(2,1)}) %all-gather.16.cloned.1.call-update) | async-done | bytes 2097168 | tf_op jit(solution)/shard_map/all_gather | solution.py:124
  850.3 29.7 %reduce-scatter.24.cloned.1.call-done = bf16[2048,256]{0,1:T(8,128)(2,1)} async-done(((bf16[2048,512]{0,1:T(8,128)(2,1)}), bf16[2048,256]{0,1:T(8,128)(2,1)}) %reduce-scatter.24.cloned.1.call-update) | async-done | bytes 1048592 | tf_op jit(solution)/shard_map/reduce_scatter | solution.py:118
  882.2 13.1 psum.207
  897.6 64.7 %while.71 = (s32[]{:T(128)}, f32[2048,64]{0,1:T(8,128)S(1)}, f32[2048,64]{0,1:T(8,128)}, f32[4,512,64]{1,0,2:T(4,128)}, s32[4]{0:T(128)}, /*index=5*/bf16[2048,6...) while((s32[]{:T(128)}, f32[2048,64]{0,1:T(8,128)S(1)}, ...), condition=%wide.region_39.40_spmd.clone, body=%wide.region_37.39_spmd.clone.sunk | while | flops 682262528 | bytes 41171244 | solution.py:196
  980.8 380.9 %while.70 = (s32[]{:T(128)}, f32[3,64,128]{2,1,0:T(8,128)}, f32[16,128,3,64]{1,0,3,2:T(8,128)}, bf16[16,128,128]{2,1,0:T(8,128)(2,1)}, bf16[16,128,128]{2,1,0:T(...) while((s32[]{:T(128)}, f32[3,64,128]{2,1,0:T(8,128)}, ...), condition=%wide.region_36.37_spmd.clone, body=%wide.region_26.36_spmd.clone.sunk | while | flops 278236544 | bytes 5056039 | solution.py:84
  1392.8 43.3 %all-reduce.32.cloned.1.call-done = (bf16[2048,128]{0,1:T(8,128)(2,1)}, bf16[2048,128]{0,1:T(8,128)(2,1)}, bf16[2048,256]{0,1:T(8,128)(2,1)}) async-done(((bf16[2048,128]{0,1:T(8,128)(2,1)}, bf16[2048,128]{0,1:T(8,128)(2,1)}, bf16[2048,256]{0,1:T(8,128)(2,1)}), (bf16[2048,128]{0,1:T(8,128)(2,1)}, bf16[2048,128]{0,1:T(8,128)(2,1)}, bf16[2048,256]{0,1:T(8,128)(2,1)})) %all-reduce.32.cloned.1.call-update) | async-done | bytes 2097168 | tf_op jit(solution)/shard_map/psum | solution.py:389
  1446.2 41.6 %all-gather.24.cloned.1.call-done = bf16[2048,896]{0,1:T(8,128)(2,1)} async-done(((bf16[2048,448]{0,1:T(8,128)(2,1)}), bf16[2048,896]{0,1:T(8,128)(2,1)}) %all-gather.24.cloned.1.call-update) | async-done | bytes 3670032 | tf_op jit(solution)/shard_map/all_gather | solution.py:394
  1521.1 20.3 %all-reduce.27 = (bf16[512,6]{0,1:T(8,128)(2,1)S(1)}, bf16[4,192]{1,0:T(4,128)(2,1)S(1)}, bf16[192]{0:T(256)(128)(2,1)S(1)}, bf16[4,256]{1,0:T(4,128)(2,1)S(1)},...) all-reduce(bf16[512,6]{0,1:T(8,128)(2,1)S(1)} %convolution_convert_, ...), channel_id=1, replica_groups=mesh['dp'=4,'row'=4,'col'=2] {'dp'}, use_global_device_ids=true, to_apply=%region_50.51 | all-reduce | flops 5513 | bytes 22052 | tf_op jit(solution)/shard_map/psum | solution.py:468
  1549.3 83.2 %all-reduce.34.cloned.1.call-done = (bf16[512,384]{1,0:T(8,128)(2,1)}, bf16[512,384]{1,0:T(8,128)(2,1)}, bf16[512,512]{1,0:T(8,128)(2,1)}, bf16[384,512]{1,0:T(8...) async-done(((bf16[512,384]{1,0:T(8,128)(2,1)}, ...) | async-done | bytes 3538960 | tf_op jit(solution)/shard_map/psum | solution.py:466
  1644.8 33.6 %reduce-scatter.26.cloned.1.call-done = f32[512,512]{1,0:T(8,128)} async-done(((f32[2048,512]{1,0:T(8,128)}), f32[512,512]{1,0:T(8,128)}) %reduce-scatter.26.cloned.1.call-update) | async-done | bytes 1048592 | tf_op jit(solution)/shard_map/reduce_scatter | solution.py:114
  1682.1 33.3 %all-reduce.25 = (f32[512]{0:T(512)}, f32[512]{0:T(512)}) all-reduce(f32[512]{0:T(512)} %get-tuple-element.829, f32[512]{0:T(512)} %get-tuple-element.823), channel_id=1, replica_groups=mesh['dp'=4,'row'=4,'col'=2] {'dp','row'}, use_global_device_ids=true, to_apply=%region_47.48 | all-reduce | flops 1024 | bytes 8192 | tf_op jit(solution)/shard_map/psum | solution.py:485
  (1512 shorter events, 854.0 us)
Async XLA Ops:
  7.2 565.8 %copy-start = (bf16[512,512]{1,0:T(8,128)(2,1)S(1)}, bf16[512,512]{1,0:T(8,128)(2,1)}, u32[]{:S(2)}) copy-start(bf16[512,512]{1,0:T(8,128)(2,1)} %param.55) | copy-start | bytes 1572868
  7.2 34.4 %all-gather.10.cloned.1.call-start = ((), (), s32[]{:S(2)}) async-start(), calls=%async_computation.9 | async-start | bytes 2621440 | tf_op jit(solution)/shard_map/all_gather | solution.py:110
  17.1 109.5 %reduce-scatter.12.cloned.1.call-start = ((), (), s32[]{:S(2)}) async-start(), calls=%async_computation.11 | async-start | bytes 9437184 | tf_op jit(solution)/shard_map/reduce_scatter | solution.py:275
  48.0 169.5 %reduce-scatter.10.cloned.1.call-start = ((), (), s32[]{:S(2)}) async-start(), calls=%async_computation.10 | async-start | bytes 11010048 | tf_op jit(solution)/shard_map/reduce_scatter | solution.py:273
  62.2 406.6 %all-gather.12.cloned.1.call-start = ((), (), s32[]{:S(2)}) async-start(), calls=%async_computation.12 | async-start | bytes 3145728 | tf_op jit(solution)/shard_map/all_gather | solution.py:124
  62.9 354.1 %copy-start.89 = (f32[192]{0:T(256)}, f32[192]{0:T(256)S(1)}, u32[]{:S(2)}) copy-start(f32[192]{0:T(256)S(1)} %mul.935) | copy-start | bytes 2308
  65.3 65.9 %copy-start.95 = (f32[1,256]{1,0:T(1,128)}, f32[1,256]{1,0:T(1,128)S(1)}, u32[]{:S(2)}) copy-start(f32[1,256]{1,0:T(1,128)S(1)} %get-tuple-element.1029) | copy-start | bytes 3076
  65.3 65.9 %copy-start.97 = (f32[1,256]{1,0:T(1,128)}, f32[1,256]{1,0:T(1,128)S(1)}, u32[]{:S(2)}) copy-start(f32[1,256]{1,0:T(1,128)S(1)} %get-tuple-element.1030) | copy-start | bytes 3076
  65.3 65.9 %copy-start.99 = (f32[1,256]{1,0:T(1,128)}, f32[1,256]{1,0:T(1,128)S(1)}, u32[]{:S(2)}) copy-start(f32[1,256]{1,0:T(1,128)S(1)} %get-tuple-element.1031) | copy-start | bytes 3076
  65.4 65.9 %copy-start.101 = (f32[1,256]{1,0:T(1,128)}, f32[1,256]{1,0:T(1,128)S(1)}, u32[]{:S(2)}) copy-start(f32[1,256]{1,0:T(1,128)S(1)} %get-tuple-element.1032) | copy-start | bytes 3076
  434.8 83.7 %reduce-scatter.14.cloned.1.call-start = ((), (), s32[]{:S(2)}) async-start(), calls=%async_computation.13 | async-start | bytes 5242880 | tf_op jit(solution)/shard_map/reduce_scatter | solution.py:114
  473.8 74.9 %all-gather.14.cloned.1.call-start = ((), (), s32[]{:S(2)}) async-start(), calls=%async_computation.14 | async-start | bytes 2621440 | tf_op jit(solution)/shard_map/all_gather | solution.py:110
  519.9 266.0 %copy-start.3 = (f32[512,512]{1,0:T(8,128)}, f32[512,512]{1,0:T(8,128)S(1)}, u32[]{:S(2)}) copy-start(f32[512,512]{1,0:T(8,128)S(1)} %get-tuple-element.947) | copy-start | bytes 3145732
  525.0 253.7 %copy-start.77 = (f32[512]{0:T(512)}, f32[512]{0:T(512)S(1)}, u32[]{:S(2)}) copy-start(f32[512]{0:T(512)S(1)} %add_rsqrt_fusion.1) | copy-start | bytes 6148
  525.9 47.0 %all-gather.18.cloned.1.call-start = ((), (), s32[]{:S(2)}) async-start(), calls=%async_computation.18 | async-start | bytes 2621440 | tf_op jit(solution)/shard_map/all_gather | solution.py:110
  526.7 103.0 %reduce-scatter.16.cloned.1.call-start = ((), (), s32[]{:S(2)}) async-start(), calls=%async_computation.15 | async-start | bytes 6291456 | tf_op jit(solution)/shard_map/reduce_scatter | solution.py:118
  554.8 109.0 %reduce-scatter.20.cloned.1.call-start = ((), (), s32[]{:S(2)}) async-start(), calls=%async_computation.19 | async-start | bytes 3145728 | tf_op jit(solution)/shard_map/reduce_scatter | solution.py:118
  577.2 150.1 %all-gather.20.cloned.1.call-start = ((), (), s32[]{:S(2)}) async-start(), calls=%async_computation.20 | async-start | bytes 6291456 | tf_op jit(solution)/shard_map/all_gather | solution.py:124
  670.4 108.2 %reduce-scatter.22.cloned.1.call-start = ((), (), s32[]{:S(2)}) async-start(), calls=%async_computation.21 | async-start | bytes 5242880 | tf_op jit(solution)/shard_map/reduce_scatter | solution.py:114
  733.9 77.4 %all-gather.22.cloned.1.call-start = ((), (), s32[]{:S(2)}) async-start(), calls=%async_computation.22 | async-start | bytes 2621440 | tf_op jit(solution)/shard_map/all_gather | solution.py:110
  788.6 57.4 %all-gather.16.cloned.1.call-start = ((), (), s32[]{:S(2)}) async-start(), calls=%async_computation.16 | async-start | bytes 3145728 | tf_op jit(solution)/shard_map/all_gather | solution.py:124
  789.4 90.6 %reduce-scatter.24.cloned.1.call-start = ((), (), s32[]{:S(2)}) async-start(), calls=%async_computation.23 | async-start | bytes 3145728 | tf_op jit(solution)/shard_map/reduce_scatter | solution.py:118
  815.6 620.5 %all-reduce.32.cloned.1.call-start = ((), (), s32[]{:S(2)}) async-start(), calls=%async_computation.26 | async-start | bytes 4194304 | tf_op jit(solution)/shard_map/psum | solution.py:389
  1373.5 114.3 %all-gather.24.cloned.1.call-start = ((), (), s32[]{:S(2)}) async-start(), calls=%async_computation.24 | async-start | bytes 5505024 | tf_op jit(solution)/shard_map/all_gather | solution.py:394
  1382.0 250.6 %all-reduce.34.cloned.1.call-start = ((), (), s32[]{:S(2)}) async-start(), calls=%async_computation.27 | async-start | bytes 7077888 | tf_op jit(solution)/shard_map/psum | solution.py:466
  1495.2 183.2 %reduce-scatter.26.cloned.1.call-start = ((), (), s32[]{:S(2)}) async-start(), calls=%async_computation.25 | async-start | bytes 5242880 | tf_op jit(solution)/shard_map/reduce_scatter | solution.py:114
  1514.8 211.0 %reduce-scatter.18.cloned.1.call-start = ((), (), s32[]{:S(2)}) async-start(), calls=%async_computation.17 | async-start | bytes 5242880 | tf_op jit(solution)/shard_map/reduce_scatter | solution.py:114
  1644.8 75.7 %copy-start.87 = (f32[512]{0:T(512)S(1)}, f32[512]{0:T(512)}, u32[]{:S(2)}) copy-start(f32[512]{0:T(512)} %copy-done.86) | copy-start | bytes 6148
  1644.8 81.0 %copy-start.4 = (f32[512,512]{1,0:T(8,128)S(1)}, f32[512,512]{1,0:T(8,128)}, u32[]{:S(2)}) copy-start(f32[512,512]{1,0:T(8,128)} %copy-done.3) | copy-start | bytes 3145732
  1644.8 81.0 %copy-start.20 = (f32[512,512]{1,0:T(8,128)S(1)}, f32[512,512]{1,0:T(8,128)}, u32[]{:S(2)}) copy-start(f32[512,512]{1,0:T(8,128)} %reduce-scatter.22.cloned.1.call-done) | copy-start | bytes 3145732
  1644.8 81.0 %copy-start.78 = (f32[512]{0:T(512)S(1)}, f32[512]{0:T(512)}, u32[]{:S(2)}) copy-start(f32[512]{0:T(512)} %copy-done.77) | copy-start | bytes 6148
  1644.8 81.0 %copy-start.83 = (f32[512]{0:T(512)S(1)}, f32[512]{0:T(512)}, u32[]{:S(2)}) copy-start(f32[512]{0:T(512)} %param.52) | copy-start | bytes 6148
  (191 other events, 1665.4 us)
Sparse Core Ops, SparseCore 0:
  17.2 24.3 all-gather.9
  48.1 78.4 reduce-scatter.11
  129.0 88.4 reduce-scatter.9
  434.9 33.9 all-gather.11
  473.9 44.4 reduce-scatter.13
  526.1 22.6 all-gather.13
  550.3 22.5 all-gather.17
  575.4 54.2 reduce-scatter.15
  631.9 31.8 reduce-scatter.19
  670.5 56.7 all-gather.19
  734.1 44.5 reduce-scatter.21
  788.7 22.5 all-gather.21
  812.9 33.1 all-gather.15
  848.1 31.8 reduce-scatter.23
  1373.6 62.5 all-reduce.31
  1437.6 50.1 all-gather.23
  1495.3 137.2 all-reduce.33
  1635.1 43.2 reduce-scatter.25
  1680.9 44.7 reduce-scatter.17
where the time goes:
time: 1750 us; the launch traced here: 1740 us
  waiting for transfers between devices  733 us (42%)
  local copies, waits for them, and re-layouts  337 us (19%)
  matrix products  297 us (17%)
  other arithmetic  218 us (12%)
  blocking collectives  116 us (7%)
  loops' own time  17.8 us (1%)
    reduce_scatter x4, waiting for transfers between devices, rows_total(): return lax.psum_scatter(values, 'row', scatter_dimension=0, tiled=True)  128 us
    all_gather x3, waiting for transfers between devices, gather_cols(): return lax.all_gather(values, 'col', axis=1, tiled=True)  118 us
    reduce_scatter x3, waiting for transfers between devices, cols_total(): lax.psum_scatter(values.astype(jnp.bfloat16), 'col', scatter_dimension=1,...  112 us
    squeeze x128, local copies, waits for them, and re-layouts, state_scan(): _, outputs = lax.scan(jax.checkpoint(advance), initial, grouped)  97.8 us
    dynamic_update_slice x32, local copies, waits for them, and re-layouts, state_scan(): _, outputs = lax.scan(jax.checkpoint(advance), initial, grouped)  93 us
    all_gather x4, waiting for transfers between devices, gather_rows(): return lax.all_gather(values, 'row', axis=0, tiled=True)  85.4 us
    psum x1, waiting for transfers between devices, local(): lax.psum(grad_w_z.astype(jnp.bfloat16), 'dp').astype(jnp.float32)  83.2 us
    reduce_scatter x1, waiting for transfers between devices, local(): lax.psum_scatter(main_term, 'col', scatter_dimension=1, tiled=True)  73 us
  transfers between devices with their start and end apart: 19, of which 19 were waited for; matrix products, arithmetic and copies ran while one was open for 8% of the time, Pallas kernels for 0%

commit v1 on v0

v1 whole, which is shorter than its diff:
```python
from functools import partial
import math

import jax
import jax.numpy as jnp
from jax import lax
from jax.experimental import pallas as pl
from jax.experimental.pallas import tpu as pltpu
from jax.sharding import PartitionSpec as P

MODEL_WIDTH = 1024
STATE_SIZE = 128
KC = 4
QUERY_HEADS = 8
KEY_VALUE_HEADS = 2
HEAD_SIZE = 64
CH = 128
QB = 512
DM = 1536


epsilon = 1e-05
rope_base = 100000000000.0
masked_score = -1e30
highest = lax.Precision.HIGHEST


def causal_conv(raw, kernel, offset):
    sequence_length = raw.shape[0]
    padded = jnp.pad(raw, ((KC - 1, 0), (0, 0)))
    summed = offset + kernel[0] * padded[0:sequence_length]
    for tap_index in range(1, KC):
        summed = summed + kernel[tap_index] * padded[tap_index : tap_index + sequence_length]
    return jax.nn.silu(summed)


def apply_rotary(values, token_positions):
    half_width = values.shape[-1] // 2
    frequency = jnp.exp(
        jnp.arange(half_width).astype(jnp.float32) * (-2.0 * math.log(rope_base) / values.shape[-1])
    )
    angle_half = token_positions[:, None] * frequency[None, :]
    angle_full = jnp.concatenate([angle_half, angle_half], axis=-1)[:, None, :]
    turned = jnp.concatenate([-values[..., half_width:], values[..., :half_width]], axis=-1)
    return values * jnp.cos(angle_full) + turned * jnp.sin(angle_full)


ROWS = ((1,), (1,))
COLS = ((0,), (0,))
VMEM_BYTES = 48 * 1024 * 1024


def dot_on(left, right, dims):
    return lax.dot_general(left, right, (dims, ((), ())), preferred_element_type=jnp.float32)


def chunk_masks():
    row = lax.broadcasted_iota(jnp.int32, (CH, CH), 0)
    column = lax.broadcasted_iota(jnp.int32, (CH, CH), 1)
    return row, column


def exact_dot(left, right, dims=((1,), (0,))):
    return lax.dot_general(
        left, right, (dims, ((), ())), precision=highest, preferred_element_type=jnp.float32
    )


def scan_forward_kernel(heads, x_ref, bc_ref, s_ref, a_ref, y_ref, start_ref, state):
    bf16 = jnp.bfloat16

    @pl.when(pl.program_id(0) == 0)
    def _():
        state[...] = jnp.zeros_like(state)

    carry = state[...]
    start_ref[0] = carry
    row, column = chunk_masks()
    causal = row >= column
    lower = jnp.where(causal, 1.0, 0.0)
    steps, decay = s_ref[...], a_ref[...]
    cum = exact_dot(lower, decay)
    cum_row = exact_dot(decay, lower, ((0,), (1,)))
    b_part, c_part = bc_ref[:, :STATE_SIZE], bc_ref[:, STATE_SIZE:]
    scores = dot_on(c_part, b_part, ROWS)
    carried = dot_on(c_part, carry.astype(bf16), ROWS)
    x_all = x_ref[...].astype(jnp.float32)
    width = x_all.shape[1] // heads
    outs, tails, ends = [], [], []
    for h in range(heads):
        span = slice(h * width, (h + 1) * width)
        c_h = cum[:, h : h + 1]
        last = cum[CH - 1 : CH, h : h + 1]
        xs = x_all[:, span] * steps[:, h : h + 1]
        within = jnp.exp(jnp.where(causal, c_h - cum_row[h : h + 1, :], masked_score))
        inside = jnp.dot(
            (within * scores).astype(bf16), xs.astype(bf16), preferred_element_type=jnp.float32
        )
        outs.append(inside + jnp.exp(c_h) * carried[:, span])
        tails.append((xs * jnp.exp(last - c_h)).astype(bf16))
        ends.append(jnp.exp(last))
    y_ref[...] = jnp.concatenate(outs, axis=1)
    update = dot_on(jnp.concatenate(tails, axis=1), b_part, COLS)
    for h in range(heads):
        span = slice(h * width, (h + 1) * width)
        state[span, :] = ends[h] * carry[span, :] + update[span, :]


def scan_backward_kernel(
    heads, x_ref, bc_ref, s_ref, a_ref, dy_ref, start_ref, dx_ref, ds_ref, da_ref, dbc_ref, dstate
):
    bf16 = jnp.bfloat16

    @pl.when(pl.program_id(0) == 0)
    def _():
        dstate[...] = jnp.zeros_like(dstate)

    dend = dstate[...]
    start = start_ref[0]
    dend_low, start_low = dend.astype(bf16), start.astype(bf16)
    row, column = chunk_masks()
    causal = row >= column
    strict = row > column
    lower = jnp.where(causal, 1.0, 0.0)
    upper = jnp.where(column >= row, 1.0, 0.0)
    upper_low = upper.astype(bf16)
    steps, decay = s_ref[...], a_ref[...]
    cum = exact_dot(lower, decay)
    cum_row = exact_dot(decay, lower, ((0,), (1,)))
    b_part, c_part = bc_ref[:, :STATE_SIZE], bc_ref[:, STATE_SIZE:]
    scores = dot_on(c_part, b_part, ROWS)
    carried = dot_on(c_part, start_low, ROWS)
    back = dot_on(b_part, dend_low, ROWS)
    x_all = x_ref[...].astype(jnp.float32)
    dy_all = dy_ref[...]
    dy_low = dy_all.astype(bf16)
    width = x_all.shape[1] // heads
    lane = lax.broadcasted_iota(jnp.int32, (CH, 8), 1)
    zero_small = jnp.zeros((CH, 8), jnp.float32)
    heads_q, heads_r, inner, ds_all = zero_small, zero_small, zero_small, zero_small
    dscores = jnp.zeros((CH, CH), jnp.float32)
    dxs_list, dye_list, tail_list, ends = [], [], [], []
    for h in range(heads):
        span = slice(h * width, (h + 1) * width)
        c_h = cum[:, h : h + 1]
        last = cum[CH - 1 : CH, h : h + 1]
        x_h = x_all[:, span]
        xs = x_h * steps[:, h : h + 1]
        dy_h = dy_all[:, span]
        e_cum = jnp.exp(c_h)
        tail = jnp.exp(last - c_h)
        within = jnp.exp(jnp.where(causal, c_h - cum_row[h : h + 1, :], masked_score))
        dmix = dot_on(dy_low[:, span], xs.astype(bf16), ROWS) * within
        dscores = dscores + dmix
        mixing = (within * scores).astype(bf16)
        back_h = tail * back[:, span]
        dxs = dot_on(mixing, dy_low[:, span], COLS) + back_h
        dye = dy_h * e_cum
        spread = jnp.dot(
            upper_low, (dmix * scores).astype(bf16), preferred_element_type=jnp.float32
        )
        end = jnp.exp(last)
        const = end * jnp.sum(
            jnp.sum(start[span, :] * dend[span, :], axis=1, keepdims=True), axis=0, keepdims=True
        )
        own = lane == h
        heads_q = jnp.where(own, jnp.sum(dye * carried[:, span], axis=1, keepdims=True), heads_q)
        heads_r = jnp.where(own, jnp.sum(xs * back_h, axis=1, keepdims=True), heads_r)
        inner = jnp.where(
            own, jnp.sum(jnp.where(strict, spread, 0.0), axis=1, keepdims=True) + const, inner
        )
        ds_all = jnp.where(own, jnp.sum(dxs * x_h, axis=1, keepdims=True), ds_all)
        dxs_list.append(dxs * steps[:, h : h + 1])
        dye_list.append(dye.astype(bf16))
        tail_list.append((xs * tail).astype(bf16))
        ends.append(end)
    dx_ref[...] = jnp.concatenate(dxs_list, axis=1)
    ds_ref[...] = ds_all
    da_ref[...] = (
        inner + exact_dot(upper, heads_q) + exact_dot(jnp.where(strict, 1.0, 0.0), heads_r)
    )
    dye_all = jnp.concatenate(dye_list, axis=1)
    dscores_low = dscores.astype(bf16)
    dbc_ref[:, :STATE_SIZE] = dot_on(dscores_low, c_part, COLS) + jnp.dot(
        jnp.concatenate(tail_list, axis=1), dend_low, preferred_element_type=jnp.float32
    )
    dbc_ref[:, STATE_SIZE:] = jnp.dot(
        dscores_low, b_part, preferred_element_type=jnp.float32
    ) + jnp.dot(dye_all, start_low, preferred_element_type=jnp.float32)
    update = dot_on(dye_all, c_part, COLS)
    for h in range(heads):
        span = slice(h * width, (h + 1) * width)
        dstate[span, :] = ends[h] * dend[span, :] + update[span, :]


def scan_forward(x_low, bc_low, steps, decay, heads):
    length, channels = x_low.shape
    chunks = length // CH
    rows = lambda width: pl.BlockSpec((CH, width), lambda i: (i, 0))
    return pl.pallas_call(
        partial(scan_forward_kernel, heads),
        grid=(chunks,),
        in_specs=[rows(channels), rows(2 * STATE_SIZE), rows(8), rows(8)],
        out_specs=[
            rows(channels),
            pl.BlockSpec((1, channels, STATE_SIZE), lambda i: (i, 0, 0)),
        ],
        out_shape=[
            jax.ShapeDtypeStruct((length, channels), jnp.float32),
            jax.ShapeDtypeStruct((chunks, channels, STATE_SIZE), jnp.float32),
        ],
        scratch_shapes=[pltpu.VMEM((channels, STATE_SIZE), jnp.float32)],
        compiler_params=pltpu.CompilerParams(vmem_limit_bytes=VMEM_BYTES),
        name="scan_forward",
    )(x_low, bc_low, steps, decay)


def scan_backward(x_low, bc_low, steps, decay, grad_out, starts, heads):
    length, channels = x_low.shape
    chunks = length // CH
    rows = lambda width: pl.BlockSpec((CH, width), lambda i: (chunks - 1 - i, 0))
    return pl.pallas_call(
        partial(scan_backward_kernel, heads),
        grid=(chunks,),
        in_specs=[
            rows(channels),
            rows(2 * STATE_SIZE),
            rows(8),
            rows(8),
            rows(channels),
            pl.BlockSpec((1, channels, STATE_SIZE), lambda i: (chunks - 1 - i, 0, 0)),
        ],
        out_specs=[rows(channels), rows(8), rows(8), rows(2 * STATE_SIZE)],
        out_shape=[
            jax.ShapeDtypeStruct((length, channels), jnp.float32),
            jax.ShapeDtypeStruct((length, 8), jnp.float32),
            jax.ShapeDtypeStruct((length, 8), jnp.float32),
            jax.ShapeDtypeStruct((length, 2 * STATE_SIZE), jnp.float32),
        ],
        scratch_shapes=[pltpu.VMEM((channels, STATE_SIZE), jnp.float32)],
        compiler_params=pltpu.CompilerParams(vmem_limit_bytes=VMEM_BYTES),
        name="scan_backward",
    )(x_low, bc_low, steps, decay, grad_out, starts)


AQ = 256


def masked_scores(q_blk, k_part, first):
    scores = dot_on(q_blk * jnp.bfloat16(HEAD_SIZE ** (-0.5)), k_part, ROWS)
    row = lax.broadcasted_iota(jnp.int32, scores.shape, 0) + first
    column = lax.broadcasted_iota(jnp.int32, scores.shape, 1)
    return jnp.where(column <= row, scores, masked_score)


def attend_forward_kernel(blocks, q_ref, k_ref, v_ref, o_ref, lse_ref):
    for index in range(blocks):

        @pl.when(pl.program_id(0) == index)
        def _(index=index):
            extent = (index + 1) * AQ
            scores = masked_scores(q_ref[...], k_ref[:extent, :], index * AQ)
            peak = jnp.max(scores, axis=1, keepdims=True)
            shifted = jnp.exp(scores - peak)
            total = jnp.sum(shifted, axis=1, keepdims=True)
            out = jnp.dot(
                shifted.astype(jnp.bfloat16), v_ref[:extent, :], preferred_element_type=jnp.float32
            )
            o_ref[...] = (out / total).astype(jnp.bfloat16)
            lse_ref[...] = peak + jnp.log(total)


def attend_backward_kernel(
    blocks, q_ref, k_ref, v_ref, g_ref, lse_ref, dq_ref, dk_ref, dv_ref
):
    scale = HEAD_SIZE ** (-0.5)

    @pl.when(pl.program_id(0) == 0)
    def _():
        dk_ref[...] = jnp.zeros_like(dk_ref)
        dv_ref[...] = jnp.zeros_like(dv_ref)

    for index in range(blocks):

        @pl.when(pl.program_id(0) == index)
        def _(index=index):
            extent = (index + 1) * AQ
            q_blk, g_blk = q_ref[...], g_ref[...]
            k_part, v_part = k_ref[:extent, :], v_ref[:extent, :]
            scores = masked_scores(q_blk, k_part, index * AQ)
            probs = jnp.exp(scores - lse_ref[...])
            grad_probs = dot_on(g_blk, v_part, ROWS)
            centre = jnp.sum(probs * grad_probs, axis=1, keepdims=True)
            grad_scores = (probs * (grad_probs - centre)).astype(jnp.bfloat16)
            dq_ref[...] = (
                jnp.dot(grad_scores, k_part, preferred_element_type=jnp.float32) * scale
            )
            dk_ref[:extent, :] += dot_on(grad_scores, q_blk, COLS) * scale
            dv_ref[:extent, :] += dot_on(probs.astype(jnp.bfloat16), g_blk, COLS)


def attend_forward(queries, key_rows, value_input):
    length = queries.shape[0]
    blocks = length // AQ
    whole = pl.BlockSpec((length, HEAD_SIZE), lambda i: (0, 0))
    part = lambda width: pl.BlockSpec((AQ, width), lambda i: (i, 0))
    return pl.pallas_call(
        partial(attend_forward_kernel, blocks),
        grid=(blocks,),
        in_specs=[part(HEAD_SIZE), whole, whole],
        out_specs=[part(HEAD_SIZE), part(1)],
        out_shape=[
            jax.ShapeDtypeStruct((length, HEAD_SIZE), jnp.bfloat16),
            jax.ShapeDtypeStruct((length, 1), jnp.float32),
        ],
        compiler_params=pltpu.CompilerParams(vmem_limit_bytes=VMEM_BYTES),
        name="attend_forward",
    )(queries, key_rows, value_input)


def attend_backward(queries, key_rows, value_input, grad_low, log_totals):
    length = queries.shape[0]
    blocks = length // AQ
    whole = pl.BlockSpec((length, HEAD_SIZE), lambda i: (0, 0))
    part = lambda width: pl.BlockSpec((AQ, width), lambda i: (i, 0))
    shape = jax.ShapeDtypeStruct((length, HEAD_SIZE), jnp.float32)
    return pl.pallas_call(
        partial(attend_backward_kernel, blocks),
        grid=(blocks,),
        in_specs=[part(HEAD_SIZE), whole, whole, part(HEAD_SIZE), part(1)],
        out_specs=[part(HEAD_SIZE), whole, whole],
        out_shape=[shape, shape, shape],
        compiler_params=pltpu.CompilerParams(vmem_limit_bytes=VMEM_BYTES),
        name="attend_backward",
    )(queries, key_rows, value_input, grad_low, log_totals)


def silu_slope(values):
    sigmoid = jax.nn.sigmoid(values)
    return sigmoid * (1.0 + values * (1.0 - sigmoid))


GRID = ("row", "col")


def swap(values):
    return lax.ppermute(values, "col", [(0, 1), (1, 0)])


def mine(values, axis):
    size = values.shape[axis] // lax.axis_size("col")
    return lax.dynamic_slice_in_dim(values, lax.axis_index("col") * size, size, axis)


def other(values, axis):
    size = values.shape[axis] // lax.axis_size("col")
    return lax.dynamic_slice_in_dim(values, (1 - lax.axis_index("col")) * size, size, axis)


def ordered(own, received, axis):
    first = lax.axis_index("col") == 0
    return jnp.concatenate(
        [jnp.where(first, own, received), jnp.where(first, received, own)], axis=axis
    )


def exchange(values, split_axis, join_axis):
    return ordered(mine(values, split_axis), swap(other(values, split_axis)), join_axis)


def gather_tokens(values):
    return lax.all_gather(values, GRID, axis=0, tiled=True)


def scatter_tokens(values):
    return lax.psum_scatter(
        values.astype(jnp.bfloat16), GRID, scatter_dimension=0, tiled=True
    ).astype(jnp.float32)


def grid_total(values):
    return lax.psum(values, GRID)


def norm_forward(values, gain):
    squares = jnp.sum(values * values, axis=-1)
    scale_row = lax.rsqrt(squares / MODEL_WIDTH + epsilon)
    return (values * scale_row[:, None] * gain, scale_row)


def norm_backward(values, scale_row, gain, grad_out):
    weighted = gain * grad_out
    inner_sum = jnp.sum(weighted * values, axis=-1)
    grad_in = (
        scale_row[:, None] * weighted - values * (scale_row**3 * inner_sum / MODEL_WIDTH)[:, None]
    )
    return (grad_in, jnp.sum(grad_out * values * scale_row[:, None], axis=0))


def dp_total(values):
    return lax.psum(values.astype(jnp.bfloat16), "dp")


def local(
    inputs,
    cotangent,
    norm_gain,
    w_z,
    w_x,
    w_dt,
    w_bc,
    conv_x,
    bias_x,
    conv_bc,
    bias_bc,
    dt_bias,
    a_log,
    d_skip,
    mixer_gain,
    out_mamba,
    w_query,
    key_matrix,
    value_matrix,
    out_attn,
    ffn_gain,
    w_gate,
    w_up,
    w_down,
):
    col_count = lax.axis_size("col")
    row_count = lax.axis_size("row")
    devices = col_count * row_count
    device_position = lax.axis_index("row") * col_count + lax.axis_index("col")
    sequence_length = inputs.shape[0] * row_count
    xw = conv_x.shape[1]
    heads = dt_bias.shape[0]
    ffn_local = w_down.shape[0] // col_count
    f32 = jnp.float32
    bf16 = jnp.bfloat16
    q_at, dt_at, s_at = 2 * xw, 2 * xw + HEAD_SIZE, 2 * xw + 2 * HEAD_SIZE

    x_float = exchange(inputs, 0, 1).astype(f32)
    pad = jnp.zeros((w_dt.shape[0], HEAD_SIZE - heads), bf16)
    sliced = [w_z, w_x, w_query, w_dt]
    shared = jnp.concatenate([w_bc, key_matrix, value_matrix], axis=1)
    own_in = jnp.concatenate([mine(w, 1) for w in sliced] + [pad, shared], axis=1)
    sent_in = jnp.concatenate([other(w, 1) for w in sliced] + [pad, shared], axis=1)
    w_all = ordered(own_in, swap(sent_in), 0)
    gains = jnp.stack([norm_gain, ffn_gain])
    gains = ordered(gains, swap(gains), 1)
    norm_gain, ffn_gain = gains[0], gains[1]
    key_value_head = device_position // (QUERY_HEADS // KEY_VALUE_HEADS)
    kv_at = s_at + 2 * STATE_SIZE
    key_at = kv_at + key_value_head * HEAD_SIZE
    value_at = key_at + KEY_VALUE_HEADS * HEAD_SIZE
    w_in = jnp.concatenate(
        [
            w_all[:, :kv_at],
            lax.dynamic_slice_in_dim(w_all, key_at, HEAD_SIZE, 1),
            lax.dynamic_slice_in_dim(w_all, value_at, HEAD_SIZE, 1),
        ],
        axis=1,
    )
    w_out = exchange(
        jnp.concatenate(
            [
                out_mamba.reshape(col_count, xw, -1),
                out_attn.reshape(col_count, HEAD_SIZE, -1),
                w_down.reshape(col_count, ffn_local, -1),
            ],
            axis=1,
        ).reshape(-1, out_mamba.shape[1]),
        0,
        1,
    )
    w_down_own = w_out[xw + HEAD_SIZE :]
    w_out = w_out[: xw + HEAD_SIZE]
    w_ffn = jnp.concatenate([mine(w_gate, 1), mine(w_up, 1)], axis=1)
    w_ffn = ordered(w_ffn, swap(jnp.concatenate([other(w_gate, 1), other(w_up, 1)], axis=1)), 0)
    cot_own = exchange(cotangent, 0, 1)

    normed, scale_one = norm_forward(x_float, norm_gain)
    normed_all = gather_tokens(normed.astype(bf16))
    cot_all = gather_tokens(cot_own)
    projected = jnp.dot(normed_all, w_in, preferred_element_type=f32)
    gate_z = projected[:, :xw]
    x_raw = projected[:, xw : 2 * xw]
    q_raw = projected[:, q_at:dt_at]
    dt_raw = projected[:, dt_at : dt_at + heads]
    bc_raw = projected[:, s_at:kv_at]
    key_unrotated = projected[:, kv_at : kv_at + HEAD_SIZE]
    value_reduced = projected[:, kv_at + HEAD_SIZE :].astype(bf16)
    x_conv, x_conv_pull = jax.vjp(causal_conv, x_raw, conv_x.astype(f32), bias_x)
    bc_conv, bc_conv_pull = jax.vjp(causal_conv, bc_raw, conv_bc.astype(f32), bias_bc)
    x_low = x_conv.astype(bf16)
    bc_low = bc_conv.astype(bf16)
    steps = jax.nn.softplus(dt_raw + dt_bias)
    log_decay = -steps * jnp.exp(a_log)
    widen = ((0, 0), (0, 8 - heads))
    steps_wide, decay_wide = jnp.pad(steps, widen), jnp.pad(log_decay, widen)
    scanned, starts = scan_forward(x_low, bc_low, steps_wide, decay_wide, heads)
    head_width = xw // heads
    skip_row = jnp.repeat(d_skip, head_width)
    ssm_out = scanned + skip_row * x_low.astype(f32)
    gated = ssm_out * jax.nn.silu(gate_z)
    mixer_scale = lax.rsqrt(grid_total(jnp.sum(gated * gated, axis=-1)) / DM + epsilon)
    mixed_low = (gated * mixer_scale[:, None] * mixer_gain).astype(bf16)
    token_positions = jnp.arange(sequence_length).astype(f32)
    qk_rot, qk_pull = jax.vjp(
        partial(apply_rotary, token_positions=token_positions),
        jnp.stack([q_raw, key_unrotated], axis=1),
    )
    q_low = qk_rot[:, 0].astype(bf16)
    k_low = qk_rot[:, 1].astype(bf16)
    attn_low, log_totals = attend_forward(q_low, k_low, value_reduced)
    joined = jnp.concatenate([mixed_low, attn_low], axis=1)
    middle = x_float + scatter_tokens(jnp.dot(joined, w_out, preferred_element_type=f32))
    normed_ffn, scale_two = norm_forward(middle, ffn_gain)
    ffn_all = gather_tokens(normed_ffn.astype(bf16))
    gate_up = jnp.dot(ffn_all, w_ffn, preferred_element_type=f32)
    gate_ffn = gate_up[:, :ffn_local]
    up_ffn = gate_up[:, ffn_local:]
    gate_silu = jax.nn.silu(gate_ffn)
    act = (gate_silu * up_ffn).astype(bf16)
    grad_act = dot_on(cot_all, w_down_own, ROWS)
    grad_gate = grad_act * up_ffn * silu_slope(gate_ffn)
    grad_up = grad_act * gate_silu
    grad_ffn = jnp.concatenate([grad_gate, grad_up], axis=1).astype(bf16)
    grad_ffn_in = scatter_tokens(dot_on(grad_ffn, w_ffn, ROWS))
    block_out = middle + scatter_tokens(jnp.dot(act, w_down_own, preferred_element_type=f32))
    block_out = exchange(block_out.astype(bf16), 1, 0)
    grad_w_ffn = dp_total(dot_on(ffn_all, grad_ffn, COLS))
    grad_w_down = dp_total(dot_on(act, cot_all, COLS))
    grad_middle_norm, grad_ffn_gain = norm_backward(middle, scale_two, ffn_gain, grad_ffn_in)
    grad_middle = cot_own.astype(f32) + grad_middle_norm
    grad_branch_all = gather_tokens(grad_middle.astype(bf16))
    grad_w_out = dp_total(dot_on(joined, grad_branch_all, COLS))
    grad_joined = dot_on(grad_branch_all, w_out, ROWS)
    grad_mixed = grad_joined[:, :xw]
    grad_attn = grad_joined[:, xw:].astype(bf16)
    weighted = mixer_gain * grad_mixed
    inner_sum = grid_total(jnp.sum(weighted * gated, axis=-1))
    grad_q_rot, grad_k_rot, value_gradient = attend_backward(
        q_low, k_low, value_reduced, grad_attn, log_totals
    )
    grad_qk = qk_pull(jnp.stack([grad_q_rot, grad_k_rot], axis=1))[0]
    grad_gated = (
        mixer_scale[:, None] * weighted - gated * (mixer_scale**3 * inner_sum / DM)[:, None]
    )
    grad_mixer_gain = jnp.sum(grad_mixed * gated * mixer_scale[:, None], axis=0)
    grad_ssm = grad_gated * jax.nn.silu(gate_z)
    grad_z = grad_gated * ssm_out * silu_slope(gate_z)
    grad_x_scan, grad_steps, grad_decay, grad_bc = scan_backward(
        x_low, bc_low, steps_wide, decay_wide, grad_ssm, starts, heads
    )
    grad_xc = grad_x_scan + skip_row * grad_ssm
    grad_d_skip = jnp.sum(
        jnp.sum(grad_ssm * x_low.astype(f32), axis=0).reshape(heads, head_width), axis=1
    )
    grad_decay = grad_decay[:, :heads]
    grad_dt = (grad_steps[:, :heads] - grad_decay * jnp.exp(a_log)) * jax.nn.sigmoid(
        dt_raw + dt_bias
    )
    grad_dt_bias = jnp.sum(grad_dt, axis=0)
    grad_a_log = jnp.sum(grad_decay * log_decay, axis=0)
    grad_x_raw, grad_conv_x, grad_bias_x = x_conv_pull(grad_xc)
    grad_bc_raw, grad_conv_bc, grad_bias_bc = bc_conv_pull(grad_bc)
    grad_in = jnp.concatenate(
        [
            grad_z,
            grad_x_raw,
            grad_qk[:, 0],
            grad_dt,
            jnp.zeros((sequence_length, HEAD_SIZE - heads), f32),
            grad_bc_raw,
            grad_qk[:, 1],
            value_gradient,
        ],
        axis=1,
    ).astype(bf16)
    grad_normed = scatter_tokens(dot_on(grad_in, w_in, ROWS))
    grad_w_in = dot_on(normed_all, grad_in, COLS)
    head_selection = (jnp.arange(KEY_VALUE_HEADS) == key_value_head).astype(f32)

    def per_head(values):
        return (head_selection[None, :, None] * values[:, None, :]).reshape(values.shape[0], -1)

    grad_w_shared = jnp.concatenate(
        [
            grad_w_in[:, s_at:kv_at],
            per_head(grad_w_in[:, kv_at : kv_at + HEAD_SIZE]),
            per_head(grad_w_in[:, kv_at + HEAD_SIZE :]),
        ],
        axis=1,
    )
    grad_w_shared = lax.psum_scatter(
        grad_w_shared.astype(bf16), ("col", "row"), scatter_dimension=0, tiled=True
    )
    grad_w_main = dp_total(grad_w_in[:, :s_at])
    grad_w_shared = lax.all_gather(lax.psum(grad_w_shared, "dp"), "row", axis=0, tiled=True)
    grad_x_norm, grad_norm_gain = norm_backward(x_float, scale_one, norm_gain, grad_normed)
    grad_inputs = exchange((grad_middle + grad_x_norm).astype(bf16), 1, 0).astype(f32)

    slot = jnp.concatenate(
        [
            grad_conv_x.reshape(-1),
            grad_bias_x,
            grad_mixer_gain,
            grad_dt_bias,
            grad_a_log,
            grad_d_skip,
        ]
    )
    common = jnp.concatenate(
        [grad_conv_bc.reshape(-1), grad_bias_bc, grad_norm_gain, grad_ffn_gain]
    )
    chosen = (jnp.arange(devices) == device_position).astype(f32)
    small = jnp.concatenate([common, (chosen[:, None] * slot[None, :]).reshape(-1)])
    small = lax.psum(small, ("dp", "row", "col"))
    common_size, slot_size = common.shape[0], slot.shape[0]
    slot = lax.dynamic_slice_in_dim(small, common_size + device_position * slot_size, slot_size, 0)
    conv_end = KC * xw
    grad_conv_x = slot[:conv_end].reshape(KC, xw)
    grad_bias_x = slot[conv_end : conv_end + xw]
    grad_mixer_gain = slot[conv_end + xw : conv_end + 2 * xw]
    tail = slot[conv_end + 2 * xw :]
    grad_dt_bias, grad_a_log, grad_d_skip = tail[:heads], tail[heads : 2 * heads], tail[2 * heads :]
    shared_width = 2 * STATE_SIZE
    grad_conv_bc = small[: KC * shared_width].reshape(KC, shared_width)
    at = KC * shared_width
    grad_bias_bc = small[at : at + shared_width]
    at = at + shared_width
    grad_norm_gain = mine(small[at : at + MODEL_WIDTH], 0)
    grad_ffn_gain = mine(small[at + MODEL_WIDTH : at + 2 * MODEL_WIDTH], 0)

    def back(values, axis):
        own, received = mine(values, axis), swap(other(values, axis))
        first = lax.axis_index("col") == 0
        left = jnp.where(first, own, received).astype(f32)
        right = jnp.where(first, received, own).astype(f32)

        def part(start, size, along):
            return jnp.concatenate(
                [lax.slice_in_dim(v, start, start + size, axis=along) for v in (left, right)],
                axis=along,
            )

        return part

    main_part = back(grad_w_main, 0)
    grad_w_z = main_part(0, xw, 1)
    grad_w_x = main_part(xw, xw, 1)
    grad_w_query = main_part(q_at, HEAD_SIZE, 1)
    grad_w_dt = main_part(dt_at, heads, 1)
    out_part = back(grad_w_out, 1)
    grad_out_mamba = out_part(0, xw, 0)
    grad_out_attn = out_part(xw, HEAD_SIZE, 0)
    ffn_part = back(grad_w_ffn, 0)
    grad_w_gate = ffn_part(0, ffn_local, 1)
    grad_w_up = ffn_part(ffn_local, ffn_local, 1)
    grad_w_down = back(grad_w_down, 1)(0, ffn_local, 0)
    grad_w_shared = grad_w_shared.astype(f32)
    kv_width = KEY_VALUE_HEADS * HEAD_SIZE
    grad_w_bc = grad_w_shared[:, :shared_width]
    key_weight_gradient = grad_w_shared[:, shared_width : shared_width + kv_width]
    value_weight_gradient = grad_w_shared[:, shared_width + kv_width :]
    return (
        block_out,
        grad_inputs,
        grad_norm_gain,
        grad_w_z,
        grad_w_x,
        grad_w_dt,
        grad_w_bc,
        grad_conv_x,
        grad_bias_x,
        grad_conv_bc,
        grad_bias_bc,
        grad_dt_bias,
        grad_a_log,
        grad_d_skip,
        grad_mixer_gain,
        grad_out_mamba,
        grad_w_query,
        key_weight_gradient,
        value_weight_gradient,
        grad_out_attn,
        grad_ffn_gain,
        grad_w_gate,
        grad_w_up,
        grad_w_down,
    )


def solution(mesh):
    in_specs = (
        P(("dp", "row"), "col"),
        P(("dp", "row"), "col"),
        P("col"),
        P("col", "row"),
        P("col", "row"),
        P("col", "row"),
        P("col", None),
        P(None, ("row", "col")),
        P(("row", "col")),
        P(),
        P(),
        P(("row", "col")),
        P(("row", "col")),
        P(("row", "col")),
        P(("row", "col")),
        P("row", "col"),
        P("col", "row"),
        P("col", None),
        P("col", None),
        P("row", "col"),
        P("col"),
        P("col", "row"),
        P("col", "row"),
        P("row", "col"),
    )
    out_specs = (
        P(("dp", "row"), "col"),
        P(("dp", "row"), "col"),
        P("col"),
        P("col", "row"),
        P("col", "row"),
        P("col", "row"),
        P("col", None),
        P(None, ("row", "col")),
        P(("row", "col")),
        P(),
        P(),
        P(("row", "col")),
        P(("row", "col")),
        P(("row", "col")),
        P(("row", "col")),
        P("row", "col"),
        P("col", "row"),
        P("col", None),
        P("col", None),
        P("row", "col"),
        P("col"),
        P("col", "row"),
        P("col", "row"),
        P("row", "col"),
    )
    return jax.shard_map(local, mesh=mesh, in_specs=in_specs, out_specs=out_specs, check_vma=False)
```

time: 1750 us -> 822 us (0.47)
  waiting for transfers between devices: 733 us -> 400 us
  local copies, waits for them, and re-layouts: 337 us -> 88.4 us
  matrix products: 297 us -> 61.3 us
  other arithmetic: 218 us -> 81 us
  Pallas kernels: 0 us -> 60.8 us
  blocking collectives: 116 us -> 73.8 us
  starting transfers between devices: 1.61 us -> 25 us
  loops' own time: 17.8 us -> 0 us
    reduce_scatter x9 -> x4, waiting for transfers between devices: 360 us -> 112 us  [scatter_tokens(): lax.psum_scatter(values.astype(jnp.bfloat16), GRID, scatter_dimension=0,...]
    dot_general x270 -> x12, matrix products: 297 us -> 61.3 us  [the longest x8 40.7 us: dot_on(): lax.dot_general(left, right, (dims, ((), ())), preferred_element_type=jnp...]
    all_gather x8 -> x4, waiting for transfers between devices: 245 us -> 58.6 us  [gather_tokens(): return lax.all_gather(values, GRID, axis=0, tiled=True)]
    dynamic_update_slice x44 -> x0, local copies, waits for them, and re-layouts: 113 us -> none  [the longest x32 93 us: state_scan(): _, outputs = lax.scan(jax.checkpoint(advance), initial, grouped)]
    squeeze x144 -> x1, local copies, waits for them, and re-layouts: 97.9 us -> 1.03 us  [local(): grad_qk[:, 1]]
    ppermute x0 -> x12, waiting for transfers between devices: none -> 92.8 us  [swap(): return lax.ppermute(values, 'col', [(0, 1), (1, 0)])]
    pallas_call x0 -> x4, Pallas kernels: none -> 60.8 us  [the longest x1 31.6 us: scan_backward(): pl.pallas_call(partial(scan_backward_kernel, heads), grid=(chunks,), in_s...]
    another operation x85 -> x7, other arithmetic: 55.9 us -> 3.95 us  [the longest x64 34.3 us: advance(): cumulative = jnp.cumsum(decay_block, axis=0)]
  transfers between devices with their start and end apart: 19 -> 22, of which waited for: 19 -> 16; matrix products, arithmetic and copies ran while one was open for 8% -> 14% of each run, Pallas kernels for 0% -> 0%
where the time goes in v1:
time: 822 us; the launch traced here: 806 us
  waiting for transfers between devices  400 us (49%)
  local copies, waits for them, and re-layouts  88.4 us (11%)
  other arithmetic  81 us (10%)
  blocking collectives  73.8 us (9%)
  matrix products  61.3 us (7%)
  Pallas kernels  60.8 us (7%)
  starting transfers between devices  25 us (3%)
  between operations  15.8 us (2%)
    reduce_scatter x4, waiting for transfers between devices, scatter_tokens(): lax.psum_scatter(values.astype(jnp.bfloat16), GRID, scatter_dimension=0,...  112 us
    psum x1, waiting for transfers between devices, local(): lax.psum(grad_w_shared, 'dp')  112 us
    ppermute x12, waiting for transfers between devices, swap(): return lax.ppermute(values, 'col', [(0, 1), (1, 0)])  92.8 us
    all_gather x4, waiting for transfers between devices, gather_tokens(): return lax.all_gather(values, GRID, axis=0, tiled=True)  58.6 us
    dot_general x8, matrix products, dot_on(): lax.dot_general(left, right, (dims, ((), ())), preferred_element_type=jnp...  40.7 us
    psum x1, blocking collectives, local(): small = lax.psum(small, ('dp', 'row', 'col'))  39.7 us
    unnamed x224, local copies, waits for them, and re-layouts  38.4 us
    pallas_call x1, Pallas kernels, scan_backward(): pl.pallas_call(partial(scan_backward_kernel, heads), grid=(chunks,), in_s...  31.6 us
  transfers between devices with their start and end apart: 22, of which 16 were waited for; matrix products, arithmetic and copies ran while one was open for 14% of the time, Pallas kernels for 0%

profile of v1, /device:TPU:0, one launch (start us, length us, event | category | flops | bytes accessed | tf_op | source)
XLA Modules:
  0.0 806.3 jit_solution(13690827029083411367)
XLA Ops:
  13.3 6.5 collective-permute-done
  40.2 4.8 fusion.38
  45.0 35.3 %collective-permute-done.3 = bf16[512,512]{0,1:T(8,128)(2,1)} collective-permute-done((bf16[512,512]{0,1:T(8,128)(2,1)}, bf16[512,512]{0,1:T(8,128)(2,1)}, u32[]{:S(2)}, u32[]{:S(2)}) %collective-permute-start.3) | collective-permute-done | bytes 524320 | tf_op jit(solution)/shard_map/ppermute | solution.py:347
  84.3 7.1 fusion.40
  103.1 11.3 %scan_forward.1 = (f32[2048,192]{1,0:T(8,128)}, f32[16,192,128]{2,1,0:T(8,128)S(1)}) custom-call(bf16[2048,192]{1,0:T(8,128)(2,1)S(1)} %get-tuple-element.175.x_ref, bf16[2048,256]{1,0:T(8,128)(2,1)S(1)} %get-tuple-element.173.bc_ref, f32[2048,8]{1,0:T(8,128)S(1)} %pad.81.s_ref, f32[2048,8]{1,0:T(8,128)S(1)} %pad.82.a_ref), custom_call_target="tpu_custom_call" | custom-call | tf_op jit(solution)/shard_map/scan_forward/pallas_call | solution.py:200
  118.7 13.1 %psum.56 = f32[2048]{0:T(1024)S(1)} all-reduce(f32[2048]{0:T(1024)S(1)} %get-tuple-element.169), channel_id=1, replica_groups=mesh['dp'=4,'row'=4,'col'=2] {'row','col'}, use_global_device_ids=true, to_apply=%region_2.3 | all-reduce | flops 2048 | bytes 16384 | tf_op jit(solution)/shard_map/psum | solution.py:382
  137.3 6.3 attend_forward.1
  148.7 52.5 %reduce-scatter.8.cloned.1.call-done = bf16[256,1024]{1,0:T(8,128)(2,1)} async-done(((bf16[2048,1024]{1,0:T(8,128)(2,1)}), bf16[256,1024]{1,0:T(8,128)(2,1)}) %reduce-scatter.8.cloned.1.call-update) | async-done | bytes 524304 | tf_op jit(solution)/shard_map/reduce_scatter | solution.py:376
  207.3 6.6 collective-permute-done.6
  216.7 10.0 %reduce-scatter.12.cloned.1.call-start = ((), (), s32[]{:S(2)}) async-start(), calls=%async_computation.10 | async-start | bytes 4718592 | tf_op jit(solution)/shard_map/reduce_scatter | solution.py:376
  241.0 10.2 %collective-permute-done.4 = bf16[512,512]{0,1:T(8,128)(2,1)} collective-permute-done((bf16[512,512]{0,1:T(8,128)(2,1)}, bf16[512,512]{0,1:T(8,128)(2,1)}, u32[]{:S(2)}, u32[]{:S(2)}) %collective-permute-start.4) | collective-permute-done | bytes 524320 | tf_op jit(solution)/shard_map/ppermute | solution.py:347
  253.7 7.0 fusion.39
  260.7 21.9 %all-gather.9.cloned.1.call-done = bf16[2048,1024]{1,0:T(8,128)(2,1)} async-done(((bf16[256,1024]{1,0:T(8,128)(2,1)}), bf16[2048,1024]{1,0:T(8,128)(2,1)}) %all-gather.9.cloned.1.call-update) | async-done | bytes 4194320 | tf_op jit(solution)/shard_map/all_gather | solution.py:372
  282.6 6.6 multiply_convert_fusion.2
  290.5 4.4 convolution_convert_fusion
  295.0 51.4 %reduce-scatter.12.cloned.1.call-done = bf16[256,1024]{1,0:T(8,128)(2,1)} async-done(((bf16[2048,1024]{1,0:T(8,128)(2,1)}), bf16[256,1024]{1,0:T(8,128)(2,1)}) %reduce-scatter.12.cloned.1.call-update) | async-done | bytes 524304 | tf_op jit(solution)/shard_map/reduce_scatter | solution.py:376
  351.6 36.6 %all-gather.11.cloned.1.call-done = bf16[2048,1024]{1,0:T(8,128)(2,1)} async-done(((bf16[256,1024]{1,0:T(8,128)(2,1)}), bf16[2048,1024]{1,0:T(8,128)(2,1)}) %all-gather.11.cloned.1.call-update) | async-done | bytes 4194320 | tf_op jit(solution)/shard_map/all_gather | solution.py:372
  394.4 13.8 %psum.57 = f32[2048]{0:T(1024)S(1)} all-reduce(f32[2048]{0:T(1024)S(1)} %get-tuple-element.143), channel_id=1, replica_groups=mesh['dp'=4,'row'=4,'col'=2] {'row','col'}, use_global_device_ids=true, to_apply=%region_9.10 | all-reduce | flops 2048 | bytes 16384 | tf_op jit(solution)/shard_map/psum | solution.py:382
  408.2 5.4 fusion.1
  413.7 31.6 %scan_backward.1 = (f32[2048,192]{1,0:T(8,128)}, f32[2048,8]{1,0:T(8,128)S(1)}, f32[2048,8]{1,0:T(8,128)S(1)}, f32[2048,256]{1,0:T(8,128)}) custom-call(bf16[2048,192]{1,0:T(8,128)(2,1)S(1)} %get-tuple-element.175.x_ref, bf16[2048,256]{1,0:T(8,128)(2,1)S(1)} %copy-done.2, f32[2048,8]{1,0:T(8,128)S(1)} %pad.81.s_ref, f32[2048,8]{1,0:T(8,128)} %copy-done, ...), custom_call_target="tpu_custom_call" | custom-call | tf_op jit(solution)/shard_map/scan_backward/pallas_call | solution.py:222
  450.6 11.7 %attend_backward.1 = (f32[2048,64]{1,0:T(8,128)S(1)}, f32[2048,64]{1,0:T(8,128)S(1)}, f32[2048,64]{1,0:T(8,128)S(1)}) custom-call(bf16[2048,64]{1,0:T(8,128)(2,1)S(1)} %copy-done.5, bf16[2048,64]{1,0:T(8,128)(2,1)S(1)} %get-tuple-element.222.k_ref, bf16[2048,64]{1,0:T(8,128)(2,1)S(1)} %copy-done.3, bf16[2048,64]{1,0:T(8,128)(2,1)S(1)} %copy-done.6, ...), custom_call_target="tpu_custom_call" | custom-call | tf_op jit(solution)/shard_map/attend_backward/pallas_call | solution.py:327
  478.2 7.7 concatenate.127
  485.8 6.9 fusion.84
  507.3 24.4 %reduce-scatter.16.cloned.1.call-done = bf16[128,512]{1,0:T(8,128)(2,1)} async-done(((bf16[1024,512]{1,0:T(8,128)(2,1)}), bf16[128,512]{1,0:T(8,128)(2,1)}) %reduce-scatter.16.cloned.1.call-update) | async-done | bytes 131088
  533.7 9.1 %convolution_convert_fusion.3 = bf16[2048,1024]{1,0:T(8,128)(2,1)} fusion(bf16[2048,896]{1,0:T(8,128)(2,1)} %concatenate.127, bf16[1024,64]{1,0:T(8,128)(2,1)S(1)} %copy-done.69, bf16[1024,64]{1,0:T(8,128)(2,1)S(1)} %copy-done.67, bf16[1024,768]{1,0:T(8,128)(2,1)} %copy-done.47), kind=kOutput, calls=%fused_computation.3 | convolution fusion | flops 3765698560 | bytes 9699328 | tf_op jit(solution)/shard_map/dot_general | solution.py:54
  550.4 112.0 %all-reduce.25.cloned.1.call-done = (bf16[128,512]{0,1:T(8,128)(2,1)}, bf16[1024,512]{0,1:T(8,128)(2,1)}, bf16[256,1024]{1,0:T(8,128)(2,1)}, bf16[1024,512]{0,1:T(8,128)(2,1)}, bf16[256,1024]{1,0:T(8,128)(2,1)}) async-done(((bf16[128,512]{0,1:T(8,128)(2,1)}, bf16[1024,512]{0,1:T(8,128)(2,1)}, bf16[256,1024]{1,0:T(8,128)(2,1)}, bf16[1024,512]{0,1:T(8,128)(2,1)}, bf16[256,1024]{1,0:T(8,128)(2,1)}), ...) | async-done | bytes 3276816 | tf_op jit(solution)/shard_map/psum | solution.py:600
  671.2 7.2 all_gather.19
  685.3 6.6 collective-permute-done.8
  691.9 19.9 %collective-permute-done.10 = bf16[512,512]{0,1:T(8,128)(2,1)} collective-permute-done((bf16[512,512]{0,1:T(8,128)(2,1)S(1)}, bf16[512,512]{0,1:T(8,128)(2,1)}, u32[]{:S(2)}, u32[]{:S(2)}) %collective-permute-start.10) | collective-permute-done | bytes 524320 | tf_op jit(solution)/shard_map/ppermute | solution.py:347
  733.4 39.7 %psum.58 = f32[12616]{0:T(1024)S(1)} all-reduce(f32[12616]{0:T(1024)} %constant_dynamic-update-slice_fusion), channel_id=1, replica_groups=mesh['dp'=4,'row'=4,'col'=2] {'dp','row','col'}, use_global_device_ids=true, to_apply=%region_29.30 | all-reduce | flops 12616 | bytes 100928 | tf_op jit(solution)/shard_map/psum | solution.py:619
  773.2 8.2 %reduce-scatter.10.cloned.1.call-done = bf16[256,1024]{1,0:T(8,128)(2,1)} async-done(((bf16[2048,1024]{1,0:T(8,128)(2,1)}), bf16[256,1024]{1,0:T(8,128)(2,1)}) %reduce-scatter.10.cloned.1.call-update) | async-done | bytes 524304 | tf_op jit(solution)/shard_map/reduce_scatter | solution.py:376
  792.6 4.5 collective-permute-done.7
  (409 shorter events, 190.2 us)
Async XLA Ops:
  7.2 77.1 %all-gather.5.cloned.1.call-start = ((), (), s32[]{:S(2)}) async-start(), calls=%async_computation.5 | async-start | bytes 4718592 | tf_op jit(solution)/shard_map/all_gather | solution.py:372
  8.0 4.6 collective-permute-start.1
  12.0 7.8 collective-permute-start
  22.6 178.7 %reduce-scatter.8.cloned.1.call-start = ((), (), s32[]{:S(2)}) async-start(), calls=%async_computation.6 | async-start | bytes 4718592 | tf_op jit(solution)/shard_map/reduce_scatter | solution.py:376
  28.2 54.3 %collective-permute-start.2 = (bf16[512,1024]{1,0:T(8,128)(2,1)}, bf16[512,1024]{1,0:T(8,128)(2,1)}, u32[]{:S(2)}, u32[]{:S(2)}) collective-permute-start(bf16[512,1024]{1,0:T(8,128)(2,1)} %concatenate.113), channel_id=1, source_target_pairs={{0,1},{1,0},{2,3},{3,2},{4,5},{5,4},{6,7},{7,6},{8,9},{9,8},{10,11... | collective-permute-start | bytes 3145736 | tf_op jit(solution)/shard_map/ppermute | solution.py:347
  32.7 47.6 %collective-permute-start.3 = (bf16[512,512]{0,1:T(8,128)(2,1)}, bf16[512,512]{0,1:T(8,128)(2,1)}, u32[]{:S(2)}, u32[]{:S(2)}) collective-permute-start(bf16[512,512]{0,1:T(8,128)(2,1)} %constant_dynamic-slice_fusion.11), channel_id=1, source_target_pairs={{0,1},{1,0},{2,3},{3,2},{4,5},{5,4},{6,7},{7,6},{8,9},{9,8},{10,11... | collective-permute-start | bytes 1572872 | tf_op jit(solution)/shard_map/ppermute | solution.py:347
  148.7 105.0 %all-gather.7.cloned.1.call-start = ((), (), s32[]{:S(2)}) async-start(), calls=%async_computation.7 | async-start | bytes 4718592 | tf_op jit(solution)/shard_map/all_gather | solution.py:372
  202.6 146.1 %copy-start.74 = (f32[256]{0:T(256)}, f32[256]{0:T(256)S(1)}, u32[]{:S(2)}) copy-start(f32[256]{0:T(256)S(1)} %add_rsqrt_fusion.1) | copy-start | bytes 3076
  204.8 77.8 %all-gather.9.cloned.1.call-start = ((), (), s32[]{:S(2)}) async-start(), calls=%async_computation.9 | async-start | bytes 4718592 | tf_op jit(solution)/shard_map/all_gather | solution.py:372
  205.8 8.1 %collective-permute-start.6 = (bf16[256,512]{1,0:T(8,128)(2,1)S(1)}, bf16[256,512]{1,0:T(8,128)(2,1)S(1)}, u32[]{:S(2)}, u32[]{:S(2)}) collective-permute-start(bf16[256,512]{1,0:T(8,128)(2,1)S(1)} %constant_dynamic-slice_fusion.5), channel_id=1, source_target_pairs={{0,1},{1,0},{2,3},{3,2},{4,5},{5,4},{6,7},{7,6},{8,9},{9,8},{10,11... | collective-permute-start | bytes 786440 | tf_op jit(solution)/shard_map/ppermute | solution.py:347
  216.7 129.8 %reduce-scatter.12.cloned.1.call-start = ((), (), s32[]{:S(2)}) async-start(), calls=%async_computation.10 | async-start | bytes 4718592 | tf_op jit(solution)/shard_map/reduce_scatter | solution.py:376
  235.8 15.4 %collective-permute-start.4 = (bf16[512,512]{0,1:T(8,128)(2,1)}, bf16[512,512]{0,1:T(8,128)(2,1)}, u32[]{:S(2)}, u32[]{:S(2)}) collective-permute-start(bf16[512,512]{0,1:T(8,128)(2,1)} %pad_maximum_fusion.23), channel_id=1, source_target_pairs={{0,1},{1,0},{2,3},{3,2},{4,5},{5,4},{6,7},{7,6},{8,9},{9,8},{10,11... | collective-permute-start | bytes 1572872 | tf_op jit(solution)/shard_map/ppermute | solution.py:347
  295.0 93.3 %all-gather.11.cloned.1.call-start = ((), (), s32[]{:S(2)}) async-start(), calls=%async_computation.11 | async-start | bytes 4718592 | tf_op jit(solution)/shard_map/all_gather | solution.py:372
  348.7 39.5 %copy-start.79 = (f32[256]{0:T(256)}, f32[256]{0:T(256)S(1)}, u32[]{:S(2)}) copy-start(f32[256]{0:T(256)S(1)} %fusion.51) | copy-start | bytes 3076
  351.4 180.4 %reduce-scatter.16.cloned.1.call-start = ((), (), s32[]{:S(2)}) async-start(), calls=%async_computation.13 | async-start | bytes 1179648
  413.6 31.6 %copy-start.19 = (f32[2048,256]{1,0:T(8,128)S(1)}, f32[2048,256]{1,0:T(8,128)}, u32[]{:S(2)}) copy-start(f32[2048,256]{1,0:T(8,128)} %copy-done.18) | copy-start | bytes 6291460
  495.4 167.0 %all-reduce.25.cloned.1.call-start = ((), (), s32[]{:S(2)}) async-start(), calls=%async_computation.14 | async-start | bytes 6553600 | tf_op jit(solution)/shard_map/psum | solution.py:600
  533.4 194.6 %reduce-scatter.14.cloned.1.call-start = ((), (), s32[]{:S(2)}) async-start(), calls=%async_computation.12 | async-start | bytes 4718592 | tf_op jit(solution)/shard_map/reduce_scatter | solution.py:376
  542.8 238.6 %reduce-scatter.10.cloned.1.call-start = ((), (), s32[]{:S(2)}) async-start(), calls=%async_computation.8 | async-start | bytes 4718592 | tf_op jit(solution)/shard_map/reduce_scatter | solution.py:376
  664.2 16.9 %collective-permute-start.11 = (bf16[256,512]{1,0:T(8,128)(2,1)}, bf16[256,512]{1,0:T(8,128)(2,1)}, u32[]{:S(2)}, u32[]{:S(2)}) collective-permute-start(bf16[256,512]{1,0:T(8,128)(2,1)} %constant_dynamic-slice_fusion), channel_id=1, source_target_pairs={{0,1},{1,0},{2,3},{3,2},{4,5},{5,4},{6,7},{7,6},{8,9},{9,8},{10,11... | collective-permute-start | bytes 786440 | tf_op jit(solution)/shard_map/ppermute | solution.py:347
  667.3 13.8 %collective-permute-start.9 = (bf16[256,512]{1,0:T(8,128)(2,1)}, bf16[256,512]{1,0:T(8,128)(2,1)}, u32[]{:S(2)}, u32[]{:S(2)}) collective-permute-start(bf16[256,512]{1,0:T(8,128)(2,1)} %constant_dynamic-slice_fusion.2), channel_id=1, source_target_pairs={{0,1},{1,0},{2,3},{3,2},{4,5},{5,4},{6,7},{7,6},{8,9},{9,8},{10,11... | collective-permute-start | bytes 786440 | tf_op jit(solution)/shard_map/ppermute | solution.py:347
  668.9 22.9 %collective-permute-start.8 = (bf16[512,512]{0,1:T(8,128)(2,1)S(1)}, bf16[512,512]{0,1:T(8,128)(2,1)}, u32[]{:S(2)}, u32[]{:S(2)}) collective-permute-start(bf16[512,512]{0,1:T(8,128)(2,1)S(1)} %constant_dynamic-slice_fusion.3), channel_id=1, source_target_pairs={{0,1},{1,0},{2,3},{3,2},{4,5},{5,4},{6,7},{7,6},{8,9},{9,8},{10,11... | collective-permute-start | bytes 1572872 | tf_op jit(solution)/shard_map/ppermute | solution.py:347
  670.5 41.3 %collective-permute-start.10 = (bf16[512,512]{0,1:T(8,128)(2,1)S(1)}, bf16[512,512]{0,1:T(8,128)(2,1)}, u32[]{:S(2)}, u32[]{:S(2)}) collective-permute-start(bf16[512,512]{0,1:T(8,128)(2,1)S(1)} %constant_dynamic-slice_fusion.1), channel_id=1, source_target_pairs={{0,1},{1,0},{2,3},{3,2},{4,5},{5,4},{6,7},{7,6},{8,9},{9,8},{10,11... | collective-permute-start | bytes 1572872 | tf_op jit(solution)/shard_map/ppermute | solution.py:347
  725.0 48.2 %copy-start.85 = (f32[256]{0:T(256)S(1)}, f32[256]{0:T(256)}, u32[]{:S(2)}) copy-start(f32[256]{0:T(256)} %copy-done.84) | copy-start | bytes 3076
  725.0 56.3 %copy-start.21 = (bf16[256,1024]{1,0:T(8,128)(2,1)S(1)}, bf16[256,1024]{1,0:T(8,128)(2,1)}, u32[]{:S(2)}) copy-start(bf16[256,1024]{1,0:T(8,128)(2,1)} %reduce-scatter.8.cloned.1.call-done) | copy-start | bytes 1572868
  725.0 56.3 %copy-start.38 = (bf16[256,1024]{1,0:T(8,128)(2,1)S(1)}, bf16[256,1024]{1,0:T(8,128)(2,1)}, u32[]{:S(2)}) copy-start(bf16[256,1024]{1,0:T(8,128)(2,1)} %reduce-scatter.12.cloned.1.call-done) | copy-start | bytes 1572868
  725.1 56.3 %copy-start.42 = (bf16[256,512]{1,0:T(8,128)(2,1)S(1)}, bf16[256,512]{1,0:T(8,128)(2,1)}, u32[]{:S(2)}) copy-start(bf16[256,512]{1,0:T(8,128)(2,1)} %copy-done.41) | copy-start | bytes 786436
  725.1 56.3 %copy-start.44 = (bf16[256,512]{1,0:T(8,128)(2,1)S(1)}, bf16[256,512]{1,0:T(8,128)(2,1)}, u32[]{:S(2)}) copy-start(bf16[256,512]{1,0:T(8,128)(2,1)} %copy-done.43) | copy-start | bytes 786436
  725.1 56.3 %copy-start.75 = (f32[256]{0:T(256)S(1)}, f32[256]{0:T(256)}, u32[]{:S(2)}) copy-start(f32[256]{0:T(256)} %copy-done.74) | copy-start | bytes 3076
  725.1 56.3 %copy-start.80 = (f32[256]{0:T(256)S(1)}, f32[256]{0:T(256)}, u32[]{:S(2)}) copy-start(f32[256]{0:T(256)} %copy-done.79) | copy-start | bytes 3076
  783.4 9.3 %collective-permute-start.5 = (bf16[256,512]{1,0:T(8,128)(2,1)S(1)}, bf16[256,512]{1,0:T(8,128)(2,1)S(1)}, u32[]{:S(2)}, u32[]{:S(2)}) collective-permute-start(bf16[256,512]{1,0:T(8,128)(2,1)S(1)} %constant_dynamic-slice_fusion.6), channel_id=1, source_target_pairs={{0,1},{1,0},{2,3},{3,2},{4,5},{5,4},{6,7},{7,6},{8,9},{9,8},{10,11... | collective-permute-start | bytes 786440 | tf_op jit(solution)/shard_map/ppermute | solution.py:347
  784.9 12.2 %collective-permute-start.7 = (bf16[256,512]{1,0:T(8,128)(2,1)S(1)}, bf16[256,512]{1,0:T(8,128)(2,1)S(1)}, u32[]{:S(2)}, u32[]{:S(2)}) collective-permute-start(bf16[256,512]{1,0:T(8,128)(2,1)S(1)} %constant_dynamic-slice_fusion.4), channel_id=1, source_target_pairs={{0,1},{1,0},{2,3},{3,2},{4,5},{5,4},{6,7},{7,6},{8,9},{9,8},{10,11... | collective-permute-start | bytes 786440 | tf_op jit(solution)/shard_map/ppermute | solution.py:347
  (91 other events, 522.3 us)
Sparse Core Ops, SparseCore 0:
  22.7 53.5 all-gather.4
  148.8 52.4 reduce-scatter.7
  204.9 38.4 all-gather.6
  245.8 36.7 all-gather.8
  295.1 51.3 reduce-scatter.11
  351.5 36.6 all-gather.10
  495.5 36.1 reduce-scatter.15
  535.6 126.7 all-reduce.24
  665.8 60.5 reduce-scatter.13
  729.9 51.3 reduce-scatter.9

commit v2 on v1

--- a/solution.py
+++ b/solution.py
@@ -429,7 +429,6 @@
 ):
     col_count = lax.axis_size("col")
     row_count = lax.axis_size("row")
-    devices = col_count * row_count
     device_position = lax.axis_index("row") * col_count + lax.axis_index("col")
     sequence_length = inputs.shape[0] * row_count
     xw = conv_x.shape[1]
@@ -461,6 +460,14 @@
         ],
         axis=1,
     )
+    cot_own = exchange(cotangent, 0, 1)
+
+    normed, scale_one = norm_forward(x_float, norm_gain)
+    normed_all = gather_tokens(normed.astype(bf16))
+    cot_all = gather_tokens(cot_own)
+    normed_all, out_mamba, out_attn, w_down, w_gate, w_up = lax.optimization_barrier(
+        (normed_all, out_mamba, out_attn, w_down, w_gate, w_up)
+    )
     w_out = exchange(
         jnp.concatenate(
             [
@@ -477,11 +484,6 @@
     w_out = w_out[: xw + HEAD_SIZE]
     w_ffn = jnp.concatenate([mine(w_gate, 1), mine(w_up, 1)], axis=1)
     w_ffn = ordered(w_ffn, swap(jnp.concatenate([other(w_gate, 1), other(w_up, 1)], axis=1)), 0)
-    cot_own = exchange(cotangent, 0, 1)
-
-    normed, scale_one = norm_forward(x_float, norm_gain)
-    normed_all = gather_tokens(normed.astype(bf16))
-    cot_all = gather_tokens(cot_own)
     projected = jnp.dot(normed_all, w_in, preferred_element_type=f32)
     gate_z = projected[:, :xw]
     x_raw = projected[:, xw : 2 * xw]
@@ -529,11 +531,11 @@
     grad_ffn_in = scatter_tokens(dot_on(grad_ffn, w_ffn, ROWS))
     block_out = middle + scatter_tokens(jnp.dot(act, w_down_own, preferred_element_type=f32))
     block_out = exchange(block_out.astype(bf16), 1, 0)
-    grad_w_ffn = dp_total(dot_on(ffn_all, grad_ffn, COLS))
-    grad_w_down = dp_total(dot_on(act, cot_all, COLS))
     grad_middle_norm, grad_ffn_gain = norm_backward(middle, scale_two, ffn_gain, grad_ffn_in)
     grad_middle = cot_own.astype(f32) + grad_middle_norm
     grad_branch_all = gather_tokens(grad_middle.astype(bf16))
+    grad_w_ffn = dp_total(dot_on(ffn_all, grad_ffn, COLS))
+    grad_w_down = dp_total(dot_on(act, cot_all, COLS))
     grad_w_out = dp_total(dot_on(joined, grad_branch_all, COLS))
     grad_joined = dot_on(grad_branch_all, w_out, ROWS)
     grad_mixed = grad_joined[:, :xw]
@@ -578,6 +580,9 @@
         ],
         axis=1,
     ).astype(bf16)
+    grad_in, grad_w_ffn, grad_w_down, grad_w_out = lax.optimization_barrier(
+        (grad_in, grad_w_ffn, grad_w_down, grad_w_out)
+    )
     grad_normed = scatter_tokens(dot_on(grad_in, w_in, ROWS))
     grad_w_in = dot_on(normed_all, grad_in, COLS)
     head_selection = (jnp.arange(KEY_VALUE_HEADS) == key_value_head).astype(f32)
@@ -614,11 +619,8 @@
     common = jnp.concatenate(
         [grad_conv_bc.reshape(-1), grad_bias_bc, grad_norm_gain, grad_ffn_gain]
     )
-    chosen = (jnp.arange(devices) == device_position).astype(f32)
-    small = jnp.concatenate([common, (chosen[:, None] * slot[None, :]).reshape(-1)])
-    small = lax.psum(small, ("dp", "row", "col"))
-    common_size, slot_size = common.shape[0], slot.shape[0]
-    slot = lax.dynamic_slice_in_dim(small, common_size + device_position * slot_size, slot_size, 0)
+    slot = dp_total(slot).astype(f32)
+    small = lax.psum(common, ("dp", "row", "col"))
     conv_end = KC * xw
     grad_conv_x = slot[:conv_end].reshape(KC, xw)
     grad_bias_x = slot[conv_end : conv_end + xw]

time: 822 us -> 844 us (1.027)
  waiting for transfers between devices: 400 us -> 450 us
  local copies, waits for them, and re-layouts: 88.4 us -> 53.4 us
  blocking collectives: 73.8 us -> 92.9 us
  starting transfers between devices: 25 us -> 16 us
    psum x1, waiting for transfers between devices: 112 us -> 7.67 us  [local(): lax.psum(grad_w_shared, 'dp')]
    reduce_scatter x4, waiting for transfers between devices: 112 us -> 190 us  [scatter_tokens(): lax.psum_scatter(values.astype(jnp.bfloat16), GRID, scatter_dimension=0,...]
    psum x0 -> x1, waiting for transfers between devices: none -> 68.1 us  [dp_total(): return lax.psum(values.astype(jnp.bfloat16), 'dp')]
    reduce_scatter x0 -> x1, waiting for transfers between devices: none -> 32 us  [local(): lax.psum_scatter(grad_w_shared.astype(bf16), ('col', 'row'), scatter_dime...]
    unnamed x11, waiting for transfers between devices: 24.6 us -> 0.18 us
    unnamed x224 -> x187, local copies, waits for them, and re-layouts: 38.4 us -> 14.1 us
    psum x1 -> x2, blocking collectives: 39.7 us -> 58.3 us  [the longest x1 45.7 us: local(): small = lax.psum(common, ('dp', 'row', 'col'))]
    all_gather x4, waiting for transfers between devices: 58.6 us -> 72.9 us  [gather_tokens(): return lax.all_gather(values, GRID, axis=0, tiled=True)]
  transfers between devices with their start and end apart: 22 -> 23, of which waited for: 16 -> 21; matrix products, arithmetic and copies ran while one was open for 14% -> 11% of each run, Pallas kernels for 0% -> 1%
where the time goes in v2:
time: 844 us; the launch traced here: 833 us
  waiting for transfers between devices  450 us (53%)
  blocking collectives  92.9 us (11%)
  other arithmetic  84 us (10%)
  Pallas kernels  60.6 us (7%)
  matrix products  60.2 us (7%)
  local copies, waits for them, and re-layouts  53.4 us (6%)
  starting transfers between devices  16 us (2%)
  between operations  15.7 us (2%)
    reduce_scatter x4, waiting for transfers between devices, scatter_tokens(): lax.psum_scatter(values.astype(jnp.bfloat16), GRID, scatter_dimension=0,...  190 us
    ppermute x12, waiting for transfers between devices, swap(): return lax.ppermute(values, 'col', [(0, 1), (1, 0)])  79.3 us
    all_gather x4, waiting for transfers between devices, gather_tokens(): return lax.all_gather(values, GRID, axis=0, tiled=True)  72.9 us
    psum x1, waiting for transfers between devices, dp_total(): return lax.psum(values.astype(jnp.bfloat16), 'dp')  68.1 us
    psum x1, blocking collectives, local(): small = lax.psum(common, ('dp', 'row', 'col'))  45.7 us
    dot_general x8, matrix products, dot_on(): lax.dot_general(left, right, (dims, ((), ())), preferred_element_type=jnp...  40.3 us
    reduce_scatter x1, waiting for transfers between devices, local(): lax.psum_scatter(grad_w_shared.astype(bf16), ('col', 'row'), scatter_dime...  32 us
    pallas_call x1, Pallas kernels, scan_backward(): pl.pallas_call(partial(scan_backward_kernel, heads), grid=(chunks,), in_s...  31.6 us
  transfers between devices with their start and end apart: 23, of which 21 were waited for; matrix products, arithmetic and copies ran while one was open for 11% of the time, Pallas kernels for 1%

profile of v2, /device:TPU:0, one launch (start us, length us, event | category | flops | bytes accessed | tf_op | source)
XLA Modules:
  0.0 833.1 jit_solution(4072472074537851566)
XLA Ops:
  13.3 6.5 collective-permute-done
  37.9 24.7 %collective-permute-done.2 = bf16[512,1024]{1,0:T(8,128)(2,1)S(1)} collective-permute-done((bf16[512,1024]{1,0:T(8,128)(2,1)}, bf16[512,1024]{1,0:T(8,128)(2,1)S(1)}, u32[]{:S(2)}, u32[]{:S(2)}) %collective-permute-start.2) | collective-permute-done | bytes 1048608 | tf_op jit(solution)/shard_map/ppermute | solution.py:347
  63.2 6.0 all-gather.5.cloned.1.call-done
  69.2 6.5 fusion.40
  87.3 11.0 %scan_forward.1 = (f32[2048,192]{1,0:T(8,128)}, f32[16,192,128]{2,1,0:T(8,128)S(1)}) custom-call(bf16[2048,192]{1,0:T(8,128)(2,1)S(1)} %get-tuple-element.150.x_ref, bf16[2048,256]{1,0:T(8,128)(2,1)S(1)} %get-tuple-element.148.bc_ref, f32[2048,8]{1,0:T(8,128)S(1)} %pad.81.s_ref, f32[2048,8]{1,0:T(8,128)S(1)} %pad.82.a_ref), custom_call_target="tpu_custom_call" | custom-call | tf_op jit(solution)/shard_map/scan_forward/pallas_call | solution.py:200
  102.6 13.7 %psum.63 = f32[2048]{0:T(1024)S(1)} all-reduce(f32[2048]{0:T(1024)S(1)} %get-tuple-element.144), channel_id=1, replica_groups=mesh['dp'=4,'row'=4,'col'=2] {'row','col'}, use_global_device_ids=true, to_apply=%region_2.3 | all-reduce | flops 2048 | bytes 16384 | tf_op jit(solution)/shard_map/psum | solution.py:382
  122.1 6.3 attend_forward.1
  128.8 6.3 collective-permute-done.3
  139.7 51.2 %reduce-scatter.6.cloned.1.call-done = bf16[256,1024]{1,0:T(8,128)(2,1)} async-done(((bf16[2048,1024]{1,0:T(8,128)(2,1)}), bf16[256,1024]{1,0:T(8,128)(2,1)}) %reduce-scatter.6.cloned.1.call-update) | async-done | bytes 524304 | tf_op jit(solution)/shard_map/reduce_scatter | solution.py:376
  196.9 6.6 collective-permute-done.6
  210.2 16.6 %collective-permute-done.4 = bf16[512,512]{1,0:T(8,128)(2,1)S(1)} collective-permute-done((bf16[512,512]{1,0:T(8,128)(2,1)S(1)}, bf16[512,512]{1,0:T(8,128)(2,1)S(1)}, u32[]{:S(2)}, u32[]{:S(2)}) %collective-permute-start.4) | collective-permute-done | bytes 524320 | tf_op jit(solution)/shard_map/ppermute | solution.py:347
  228.0 6.4 all-gather.7.cloned.1.call-done
  234.4 6.8 fusion.39
  241.2 32.4 %all-gather.9.cloned.1.call-done = bf16[2048,1024]{1,0:T(8,128)(2,1)} async-done(((bf16[256,1024]{1,0:T(8,128)(2,1)}), bf16[2048,1024]{1,0:T(8,128)(2,1)}) %all-gather.9.cloned.1.call-update) | async-done | bytes 4194320 | tf_op jit(solution)/shard_map/all_gather | solution.py:372
  273.6 6.6 multiply_convert_fusion.2
  286.1 51.4 %reduce-scatter.10.cloned.1.call-done = bf16[256,1024]{1,0:T(8,128)(2,1)} async-done(((bf16[2048,1024]{1,0:T(8,128)(2,1)}), bf16[256,1024]{1,0:T(8,128)(2,1)}) %reduce-scatter.10.cloned.1.call-update) | async-done | bytes 524304 | tf_op jit(solution)/shard_map/reduce_scatter | solution.py:376
  350.6 28.1 %all-gather.11.cloned.1.call-done = bf16[2048,1024]{1,0:T(8,128)(2,1)} async-done(((bf16[256,1024]{1,0:T(8,128)(2,1)}), bf16[2048,1024]{1,0:T(8,128)(2,1)}) %all-gather.11.cloned.1.call-update) | async-done | bytes 4194320 | tf_op jit(solution)/shard_map/all_gather | solution.py:372
  384.8 13.8 %psum.64 = f32[2048]{0:T(1024)S(1)} all-reduce(f32[2048]{0:T(1024)S(1)} %get-tuple-element.115), channel_id=1, replica_groups=mesh['dp'=4,'row'=4,'col'=2] {'row','col'}, use_global_device_ids=true, to_apply=%region_9.10 | all-reduce | flops 2048 | bytes 16384 | tf_op jit(solution)/shard_map/psum | solution.py:382
  404.1 31.6 %scan_backward.1 = (f32[2048,192]{1,0:T(8,128)}, f32[2048,8]{1,0:T(8,128)S(1)}, f32[2048,8]{1,0:T(8,128)S(1)}, f32[2048,256]{1,0:T(8,128)}) custom-call(bf16[2048,192]{1,0:T(8,128)(2,1)S(1)} %get-tuple-element.150.x_ref, bf16[2048,256]{1,0:T(8,128)(2,1)S(1)} %copy-done.2, f32[2048,8]{1,0:T(8,128)S(1)} %pad.81.s_ref, f32[2048,8]{1,0:T(8,128)} %copy-done, ...), custom_call_target="tpu_custom_call" | custom-call | tf_op jit(solution)/shard_map/scan_backward/pallas_call | solution.py:222
  443.4 11.8 %attend_backward.1 = (f32[2048,64]{1,0:T(8,128)S(1)}, f32[2048,64]{1,0:T(8,128)S(1)}, f32[2048,64]{1,0:T(8,128)S(1)}) custom-call(bf16[2048,64]{1,0:T(8,128)(2,1)S(1)} %copy-done.5, bf16[2048,64]{1,0:T(8,128)(2,1)S(1)} %get-tuple-element.197.k_ref, bf16[2048,64]{1,0:T(8,128)(2,1)S(1)} %copy-done.3, bf16[2048,64]{1,0:T(8,128)(2,1)S(1)} %copy-done.6, ...), custom_call_target="tpu_custom_call" | custom-call | tf_op jit(solution)/shard_map/attend_backward/pallas_call | solution.py:327
  481.2 7.8 concatenate.128
  489.0 68.1 %all-reduce.29.cloned.1.call-done = (bf16[1024,512]{1,0:T(8,128)(2,1)}, bf16[256,1024]{1,0:T(8,128)(2,1)}, bf16[256,1024]{1,0:T(8,128)(2,1)}) async-done(((bf16[1024,512]{1,0:T(8,128)(2,1)}, bf16[256,1024]{1,0:T(8,128)(2,1)}, bf16[256,1024]{1,0:T(8,128)(2,1)}), (bf16[1024,512]{1,0:T(8,128)(2,1)}, bf16[256,1024]{1,0:T(8,128)(2,1)}, bf16[256,1024]{1,0:T(8,128)(2,1)})) %all-reduce.29.cloned.1.call-update) | async-done | bytes 2097168 | tf_op jit(solution)/shard_map/psum | solution.py:401
  557.0 6.9 fusion.82
  570.7 32.0 %reduce-scatter.14.cloned.1.call-done = bf16[128,512]{1,0:T(8,128)(2,1)} async-done(((bf16[1024,512]{1,0:T(8,128)(2,1)}), bf16[128,512]{1,0:T(8,128)(2,1)}) %reduce-scatter.14.cloned.1.call-update) | async-done | bytes 131088 | tf_op jit(solution)/shard_map/reduce_scatter | solution.py:601
  602.8 8.3 convolution_convert_fusion.3
  616.4 12.5 %psum.71 = bf16[1161]{0:T(1024)(128)(2,1)S(1)} all-reduce(bf16[1161]{0:T(1024)(128)(2,1)S(1)} %concatenate.135), channel_id=1, replica_groups=mesh['dp'=4,'row'=4,'col'=2] {'dp'}, use_global_device_ids=true, to_apply=%region_36.37 | all-reduce | flops 1161 | bytes 4644 | tf_op jit(solution)/shard_map/psum | solution.py:401
  639.6 5.6 collective-permute-done.9
  654.7 7.7 all-reduce.27.cloned.1.call-done
  666.2 7.1 all_gather.19
  682.4 34.5 %reduce-scatter.12.cloned.1.call-done = bf16[256,1024]{1,0:T(8,128)(2,1)} async-done(((bf16[2048,1024]{1,0:T(8,128)(2,1)}), bf16[256,1024]{1,0:T(8,128)(2,1)}) %reduce-scatter.12.cloned.1.call-update) | async-done | bytes 524304 | tf_op jit(solution)/shard_map/reduce_scatter | solution.py:376
  718.3 53.3 %reduce-scatter.8.cloned.1.call-done = bf16[256,1024]{1,0:T(8,128)(2,1)} async-done(((bf16[2048,1024]{1,0:T(8,128)(2,1)}), bf16[256,1024]{1,0:T(8,128)(2,1)}) %reduce-scatter.8.cloned.1.call-update) | async-done | bytes 524304 | tf_op jit(solution)/shard_map/reduce_scatter | solution.py:376
  775.8 45.7 %psum.68 = f32[3328]{0:T(1024)S(1)} all-reduce(f32[3328]{0:T(1024)S(1)} %pad_maximum_fusion.32), channel_id=1, replica_groups=mesh['dp'=4,'row'=4,'col'=2] {'dp','row','col'}, use_global_device_ids=true, to_apply=%region_22.23 | all-reduce | flops 3328 | bytes 26624 | tf_op jit(solution)/shard_map/psum | solution.py:623
  (375 shorter events, 183.6 us)
Async XLA Ops:
  7.2 61.9 %all-gather.5.cloned.1.call-start = ((), (), s32[]{:S(2)}) async-start(), calls=%async_computation.5 | async-start | bytes 4718592 | tf_op jit(solution)/shard_map/all_gather | solution.py:372
  8.0 4.6 collective-permute-start.1
  12.0 7.8 collective-permute-start
  22.5 168.3 %reduce-scatter.6.cloned.1.call-start = ((), (), s32[]{:S(2)}) async-start(), calls=%async_computation.6 | async-start | bytes 4718592 | tf_op jit(solution)/shard_map/reduce_scatter | solution.py:376
  26.8 35.8 %collective-permute-start.2 = (bf16[512,1024]{1,0:T(8,128)(2,1)}, bf16[512,1024]{1,0:T(8,128)(2,1)S(1)}, u32[]{:S(2)}, u32[]{:S(2)}) collective-permute-start(bf16[512,1024]{1,0:T(8,128)(2,1)} %concatenate.114), channel_id=1, source_target_pairs={{0,1},{1,0},{2,3},{3,2},{4,5},{5,4},{6,7},{7,6},{8,9},{9,8},{10,11... | collective-permute-start | bytes 3145736 | tf_op jit(solution)/shard_map/ppermute | solution.py:347
  121.2 13.9 %collective-permute-start.3 = (bf16[512,512]{1,0:T(8,128)(2,1)S(1)}, bf16[512,512]{1,0:T(8,128)(2,1)S(1)}, u32[]{:S(2)}, u32[]{:S(2)}) collective-permute-start(bf16[512,512]{1,0:T(8,128)(2,1)S(1)} %constant_dynamic-slice_fusion.11), channel_id=1, source_target_pairs={{0,1},{1,0},{2,3},{3,2},{4,5},{5,4},{6,7},{7,6},{8,9},{9,8},{10,11... | collective-permute-start | bytes 1572872 | tf_op jit(solution)/shard_map/ppermute | solution.py:347
  139.6 94.8 %all-gather.7.cloned.1.call-start = ((), (), s32[]{:S(2)}) async-start(), calls=%async_computation.7 | async-start | bytes 4718592 | tf_op jit(solution)/shard_map/all_gather | solution.py:372
  194.4 79.2 %all-gather.9.cloned.1.call-start = ((), (), s32[]{:S(2)}) async-start(), calls=%async_computation.9 | async-start | bytes 4718592 | tf_op jit(solution)/shard_map/all_gather | solution.py:372
  195.4 8.1 collective-permute-start.6
  206.3 131.2 %reduce-scatter.10.cloned.1.call-start = ((), (), s32[]{:S(2)}) async-start(), calls=%async_computation.10 | async-start | bytes 4718592 | tf_op jit(solution)/shard_map/reduce_scatter | solution.py:376
  208.7 18.1 %collective-permute-start.4 = (bf16[512,512]{1,0:T(8,128)(2,1)S(1)}, bf16[512,512]{1,0:T(8,128)(2,1)S(1)}, u32[]{:S(2)}, u32[]{:S(2)}) collective-permute-start(bf16[512,512]{1,0:T(8,128)(2,1)S(1)} %pad_maximum_fusion.23), channel_id=1, source_target_pairs={{0,1},{1,0},{2,3},{3,2},{4,5},{5,4},{6,7},{7,6},{8,9},{9,8},{10,11... | collective-permute-start | bytes 1572872 | tf_op jit(solution)/shard_map/ppermute | solution.py:347
  286.0 92.7 %all-gather.11.cloned.1.call-start = ((), (), s32[]{:S(2)}) async-start(), calls=%async_computation.11 | async-start | bytes 4718592 | tf_op jit(solution)/shard_map/all_gather | solution.py:372
  341.8 215.2 %all-reduce.29.cloned.1.call-start = ((), (), s32[]{:S(2)}) async-start(), calls=%async_computation.15 | async-start | bytes 4194304 | tf_op jit(solution)/shard_map/psum | solution.py:401
  469.2 133.5 %reduce-scatter.14.cloned.1.call-start = ((), (), s32[]{:S(2)}) async-start(), calls=%async_computation.13 | async-start | bytes 1179648 | tf_op jit(solution)/shard_map/reduce_scatter | solution.py:601
  567.6 94.8 %all-reduce.27.cloned.1.call-start = ((), (), s32[]{:S(2)}) async-start(), calls=%async_computation.14 | async-start | bytes 2359296 | tf_op jit(solution)/shard_map/psum | solution.py:605
  569.4 33.4 %copy-start.53 = (bf16[1024,768]{1,0:T(8,128)(2,1)S(1)}, bf16[1024,768]{1,0:T(8,128)(2,1)}, u32[]{:S(2)}) copy-start(bf16[1024,768]{1,0:T(8,128)(2,1)} %copy-done.52) | copy-start | bytes 4718596
  569.4 33.4 %copy-start.70 = (bf16[1024,64]{1,0:T(8,128)(2,1)S(1)}, bf16[1024,64]{1,0:T(8,128)(2,1)}, u32[]{:S(2)}) copy-start(bf16[1024,64]{1,0:T(8,128)(2,1)} %copy-done.69) | copy-start | bytes 393220
  569.4 33.4 %copy-start.72 = (bf16[1024,64]{1,0:T(8,128)(2,1)S(1)}, bf16[1024,64]{1,0:T(8,128)(2,1)}, u32[]{:S(2)}) copy-start(bf16[1024,64]{1,0:T(8,128)(2,1)} %copy-done.71) | copy-start | bytes 393220
  602.7 114.2 %reduce-scatter.12.cloned.1.call-start = ((), (), s32[]{:S(2)}) async-start(), calls=%async_computation.12 | async-start | bytes 4718592 | tf_op jit(solution)/shard_map/reduce_scatter | solution.py:376
  611.1 160.5 %reduce-scatter.8.cloned.1.call-start = ((), (), s32[]{:S(2)}) async-start(), calls=%async_computation.8 | async-start | bytes 4718592 | tf_op jit(solution)/shard_map/reduce_scatter | solution.py:376
  630.3 9.3 %collective-permute-start.11 = (bf16[256,512]{1,0:T(8,128)(2,1)S(1)}, bf16[256,512]{1,0:T(8,128)(2,1)S(1)}, u32[]{:S(2)}, u32[]{:S(2)}) collective-permute-start(bf16[256,512]{1,0:T(8,128)(2,1)S(1)} %constant_dynamic-slice_fusion), channel_id=1, source_target_pairs={{0,1},{1,0},{2,3},{3,2},{4,5},{5,4},{6,7},{7,6},{8,9},{9,8},{10,11... | collective-permute-start | bytes 786440 | tf_op jit(solution)/shard_map/ppermute | solution.py:347
  631.8 13.4 %collective-permute-start.9 = (bf16[256,512]{1,0:T(8,128)(2,1)S(1)}, bf16[256,512]{1,0:T(8,128)(2,1)S(1)}, u32[]{:S(2)}, u32[]{:S(2)}) collective-permute-start(bf16[256,512]{1,0:T(8,128)(2,1)S(1)} %constant_dynamic-slice_fusion.2), channel_id=1, source_target_pairs={{0,1},{1,0},{2,3},{3,2},{4,5},{5,4},{6,7},{7,6},{8,9},{9,8},{10,11... | collective-permute-start | bytes 786440 | tf_op jit(solution)/shard_map/ppermute | solution.py:347
  633.1 20.1 %collective-permute-start.10 = (bf16[512,512]{1,0:T(8,128)(2,1)S(1)}, bf16[512,512]{1,0:T(8,128)(2,1)S(1)}, u32[]{:S(2)}, u32[]{:S(2)}) collective-permute-start(bf16[512,512]{1,0:T(8,128)(2,1)S(1)} %constant_dynamic-slice_fusion.1), channel_id=1, source_target_pairs={{0,1},{1,0},{2,3},{3,2},{4,5},{5,4},{6,7},{7,6},{8,9},{9,8},{10,11... | collective-permute-start | bytes 1572872 | tf_op jit(solution)/shard_map/ppermute | solution.py:347
  663.5 13.9 %collective-permute-start.8 = (bf16[512,512]{1,0:T(8,128)(2,1)S(1)}, bf16[512,512]{1,0:T(8,128)(2,1)S(1)}, u32[]{:S(2)}, u32[]{:S(2)}) collective-permute-start(bf16[512,512]{1,0:T(8,128)(2,1)S(1)} %constant_dynamic-slice_fusion.3), channel_id=1, source_target_pairs={{0,1},{1,0},{2,3},{3,2},{4,5},{5,4},{6,7},{7,6},{8,9},{9,8},{10,11... | collective-permute-start | bytes 1572872 | tf_op jit(solution)/shard_map/ppermute | solution.py:347
  680.2 36.7 %copy-start.15 = (bf16[256,512]{1,0:T(8,128)(2,1)S(1)}, bf16[256,512]{1,0:T(8,128)(2,1)}, u32[]{:S(2)}) copy-start(bf16[256,512]{1,0:T(8,128)(2,1)} %copy-done.14) | copy-start | bytes 786436
  680.2 38.1 %copy-start.77 = (f32[256]{0:T(256)S(1)}, f32[256]{0:T(256)}, u32[]{:S(2)}) copy-start(f32[256]{0:T(256)} %copy-done.76) | copy-start | bytes 3076
  680.2 91.4 %copy-start.21 = (bf16[256,1024]{1,0:T(8,128)(2,1)S(1)}, bf16[256,1024]{1,0:T(8,128)(2,1)}, u32[]{:S(2)}) copy-start(bf16[256,1024]{1,0:T(8,128)(2,1)} %reduce-scatter.6.cloned.1.call-done) | copy-start | bytes 1572868
  680.2 91.4 %copy-start.41 = (bf16[256,1024]{1,0:T(8,128)(2,1)S(1)}, bf16[256,1024]{1,0:T(8,128)(2,1)}, u32[]{:S(2)}) copy-start(bf16[256,1024]{1,0:T(8,128)(2,1)} %reduce-scatter.10.cloned.1.call-done) | copy-start | bytes 1572868
  680.2 91.4 %copy-start.46 = (bf16[256,512]{1,0:T(8,128)(2,1)S(1)}, bf16[256,512]{1,0:T(8,128)(2,1)}, u32[]{:S(2)}) copy-start(bf16[256,512]{1,0:T(8,128)(2,1)} %copy-done.45) | copy-start | bytes 786436
  680.2 91.4 %copy-start.48 = (bf16[256,512]{1,0:T(8,128)(2,1)S(1)}, bf16[256,512]{1,0:T(8,128)(2,1)}, u32[]{:S(2)}) copy-start(bf16[256,512]{1,0:T(8,128)(2,1)} %copy-done.47) | copy-start | bytes 786436
  773.6 50.4 %collective-permute-start.5 = (bf16[256,512]{1,0:T(8,128)(2,1)S(1)}, bf16[256,512]{1,0:T(8,128)(2,1)S(1)}, u32[]{:S(2)}, u32[]{:S(2)}) collective-permute-start(bf16[256,512]{1,0:T(8,128)(2,1)S(1)} %constant_dynamic-slice_fusion.6), channel_id=1, source_target_pairs={{0,1},{1,0},{2,3},{3,2},{4,5},{5,4},{6,7},{7,6},{8,9},{9,8},{10,11... | collective-permute-start | bytes 786440 | tf_op jit(solution)/shard_map/ppermute | solution.py:347
  775.1 48.9 %collective-permute-start.7 = (bf16[256,512]{1,0:T(8,128)(2,1)S(1)}, bf16[256,512]{1,0:T(8,128)(2,1)S(1)}, u32[]{:S(2)}, u32[]{:S(2)}) collective-permute-start(bf16[256,512]{1,0:T(8,128)(2,1)S(1)} %constant_dynamic-slice_fusion.4), channel_id=1, source_target_pairs={{0,1},{1,0},{2,3},{3,2},{4,5},{5,4},{6,7},{7,6},{8,9},{9,8},{10,11... | collective-permute-start | bytes 786440 | tf_op jit(solution)/shard_map/ppermute | solution.py:347
  (82 other events, 529.6 us)
Sparse Core Ops, SparseCore 0:
  22.7 46.4 all-gather.4
  139.8 51.0 reduce-scatter.5
  194.5 39.8 all-gather.6
  236.9 36.7 all-gather.8
  286.1 51.3 reduce-scatter.9
  341.9 36.6 all-gather.10
  469.3 87.6 all-reduce.28
  567.7 34.9 reduce-scatter.13
  605.9 56.4 all-reduce.26
  666.0 50.8 reduce-scatter.11
  720.3 51.2 reduce-scatter.7
